TPU v7x, 128 devices: a whole 4x4x4 slice. The times are simulated.
128 devices in a mesh: section: 8 (over x_lo, z), dp: 16 (over y, x_hi, core).
Axes of the slice: x: 4 (x_hi: 2, x_lo: 2; x = x_hi * 2 + x_lo), y: 4, z: 4, core: 2. Of those that a mesh axis runs over, the one named last changes fastest.
Arguments:
- tokens: bfloat16 [5120, 3072], P('dp'), may hold values from -6 to 6
- cotangent: bfloat16 [5120, 3072], P('dp'), may hold values from -6 to 6
- live_counts: int32 [16, 4], P('dp'), may hold values from 1 to 80, 240 in all within a row
- weight: bfloat16 [8, 3072, 3072], P('section'), may hold values from -0.0546875 to 0.0546875
- inverse_in: float32 [8, 16, 192, 192], P('section', 'dp'), may hold values from -3 to 4, as said below
- inverse_out: float32 [8, 16, 192, 192], P('section'), may hold values from -3 to 4, as said below
Outputs:
- update: bfloat16 [8, 3072, 3072], P('section', 'dp')
- factor_in: float32 [8, 16, 192, 192], P('section', 'dp')
- factor_out: float32 [8, 16, 192, 192], P('section', 'dp')
Inputs may be any that keep to these rules, and one draw needn't show every extreme that they name: `live_counts`: on each data rank the live counts of the micro-batches sum to 240, and one of them is 80. `inverse_in`: each block is symmetric. `inverse_out`: each block is symmetric.
All inputs are finite; a program needn't handle non-finite values.
Results may differ from a plain program's by a relative error of at most 0.025.
Values may be sent and summed in bfloat16 or wider, within the bound.
A program may use at most 192 MiB of HBM per device.

v0:
```python
import jax
import jax.numpy as jnp
from jax import lax
from jax.sharding import PartitionSpec as P

D = 3072
BLOCK = 192
MICRO = 4
ROWS = 80
TOK_DEV = 320
NBLK = 16


C_ZERO = 0.7978845608028654
C_ONE = 0.044715


def from_behind(x, axis, by):
    peers = lax.axis_size(axis)
    pairs = [(i, i + by) for i in range(peers) if 0 <= i + by < peers]
    return lax.ppermute(x, axis, pairs)


def activate(value):
    return 0.5 * value * (1.0 + jnp.tanh(C_ZERO * (value + C_ONE * value * value * value)))


def slope(value):
    hyper = jnp.tanh(C_ZERO * (value + C_ONE * value * value * value))
    return 0.5 * (1.0 + hyper) + 0.5 * value * (1.0 - hyper * hyper) * C_ZERO * (
        1.0 + 3.0 * C_ONE * value * value
    )


def block_gram(rows_data, total):
    blocks = rows_data.reshape(rows_data.shape[0], NBLK, BLOCK)
    return jnp.einsum("tkb,tkc->kbc", blocks, blocks, preferred_element_type=jnp.float32) / total


def shards(tokens, cotangent, live_counts, weight, inverse_in, inverse_out):
    section_count = lax.axis_size("section")
    section_here = lax.axis_index("section")
    rank_count = lax.axis_size("dp")
    matrix = weight[0]
    counts = live_counts[0]
    slots = jnp.arange(ROWS, dtype=jnp.int32)
    live = (slots[None, :] < counts[:, None]).astype(jnp.float32)[:, :, None]
    input_blocks = tokens.reshape(MICRO, ROWS, D)
    cot_blocks = cotangent.reshape(MICRO, ROWS, D)
    ticks = MICRO + section_count - 1
    total = jnp.float32(TOK_DEV * rank_count)

    def forward_tick(tick, carry):
        outgoing, stored_in, stored_pre = carry
        arrived = from_behind(outgoing, "section", 1)
        micro = tick - section_here
        valid = jnp.logical_and(micro >= 0, micro < MICRO)
        index = jnp.clip(micro, 0, MICRO - 1)
        first = lax.dynamic_index_in_dim(input_blocks, index, 0, keepdims=False)
        current = jnp.where(section_here == 0, first, arrived)
        pre = lax.cond(
            valid,
            lambda v: jnp.dot(v, matrix, preferred_element_type=jnp.float32),
            lambda v: jnp.zeros((ROWS, D), jnp.float32),
            current,
        )
        result = (current.astype(jnp.float32) + activate(pre)).astype(jnp.bfloat16)
        old_in = lax.dynamic_index_in_dim(stored_in, index, 0, keepdims=False)
        old_pre = lax.dynamic_index_in_dim(stored_pre, index, 0, keepdims=False)
        stored_in = lax.dynamic_update_index_in_dim(
            stored_in, jnp.where(valid, current, old_in), index, 0
        )
        stored_pre = lax.dynamic_update_index_in_dim(
            stored_pre, jnp.where(valid, pre, old_pre), index, 0
        )
        return (result, stored_in, stored_pre)

    start_fwd = (
        jnp.zeros((ROWS, D), jnp.bfloat16),
        jnp.zeros((MICRO, ROWS, D), jnp.bfloat16),
        jnp.zeros((MICRO, ROWS, D), jnp.float32),
    )
    unused, stored_in, stored_pre = lax.fori_loop(0, ticks, forward_tick, start_fwd)
    in_flat = stored_in.reshape(TOK_DEV, D)
    live_in = (stored_in * live.astype(jnp.bfloat16)).reshape(TOK_DEV, D)
    gram_in = block_gram(live_in, total)

    def backward_tick(tick, carry):
        outgoing, stored_scaled = carry
        arrived = from_behind(outgoing, "section", -1)
        micro = tick - (section_count - 1 - section_here)
        valid = jnp.logical_and(micro >= 0, micro < MICRO)
        index = jnp.clip(micro, 0, MICRO - 1)
        last = lax.dynamic_index_in_dim(cot_blocks, index, 0, keepdims=False)
        current = jnp.where(section_here == section_count - 1, last, arrived)
        pre = lax.dynamic_index_in_dim(stored_pre, index, 0, keepdims=False)
        mask = lax.dynamic_index_in_dim(live, index, 0, keepdims=False)
        scaled = (current.astype(jnp.float32) * slope(pre) * mask).astype(jnp.bfloat16)
        back = lax.cond(
            valid,
            lambda v: lax.dot_general(
                v, matrix, (((1,), (1,)), ((), ())), preferred_element_type=jnp.float32
            ),
            lambda v: jnp.zeros((ROWS, D), jnp.float32),
            scaled,
        )
        result = (current.astype(jnp.float32) + back).astype(jnp.bfloat16)
        old = lax.dynamic_index_in_dim(stored_scaled, index, 0, keepdims=False)
        stored_scaled = lax.dynamic_update_index_in_dim(
            stored_scaled, jnp.where(valid, scaled, old), index, 0
        )
        return (result, stored_scaled)

    start_bwd = (jnp.zeros((ROWS, D), jnp.bfloat16), jnp.zeros((MICRO, ROWS, D), jnp.bfloat16))
    unused_flow, stored_scaled = lax.fori_loop(0, ticks, backward_tick, start_bwd)
    scaled_flat = stored_scaled.reshape(TOK_DEV, D)
    gram_out = block_gram(scaled_flat, total)
    owned_in, owned_out = (
        lax.psum_scatter(
            gram_in.astype(jnp.bfloat16), "dp", scatter_dimension=0, tiled=True
        ).astype(jnp.float32),
        lax.psum_scatter(
            gram_out.astype(jnp.bfloat16), "dp", scatter_dimension=0, tiled=True
        ).astype(jnp.float32),
    )
    owned_rows = D // rank_count
    left = in_flat
    grad_rows = lax.psum_scatter(
        lax.dot_general(
            left, scaled_flat, (((0,), (0,)), ((), ())), preferred_element_type=jnp.float32
        ).astype(jnp.bfloat16),
        "dp",
        scatter_dimension=0,
        tiled=True,
    ).astype(jnp.float32)
    left = jnp.einsum(
        "kbc,kcd->kbd",
        inverse_in[0],
        grad_rows.reshape(owned_rows // BLOCK, BLOCK, D),
        precision=lax.Precision.HIGHEST,
    )
    right = jnp.einsum(
        "rkc,kce->rke",
        left.reshape(owned_rows, NBLK, BLOCK),
        inverse_out[0],
        precision=lax.Precision.HIGHEST,
    )
    update = (right.reshape(owned_rows, D) / jnp.sqrt(total)).astype(jnp.bfloat16)
    return (update[None], owned_in[None], owned_out[None])


def solution(mesh):
    in_specs = (
        P("dp", None),
        P("dp", None),
        P("dp", None),
        P("section", None, None),
        P("section", "dp", None, None),
        P("section", None, None, None),
    )
    out_specs = (
        P("section", "dp", None),
        P("section", "dp", None, None),
        P("section", "dp", None, None),
    )
    return jax.shard_map(shards, mesh=mesh, in_specs=in_specs, out_specs=out_specs, check_vma=False)
```

profile of v0, /device:TPU:5, one launch (start us, length us, event | category | flops | bytes accessed | tf_op | source)
XLA Modules:
  0.0 978.0 jit_solution(14084459570772074521)
XLA Ops:
  11.9 290.2 %while.37 = (s32[]{:T(128)}, bf16[80,3072]{1,0:T(8,128)(2,1)}, bf16[4,80,3072]{2,1,0:T(8,128)(2,1)}, f32[4,80,3072]{2,1,0:T(8,128)}, pred[]{:T(512)}, /*index=5*...) while((s32[]{:T(128)}, bf16[80,3072]{1,0:T(8,128)(2,1)}, ...), condition=%wide.region_3.4_spmd.clone, body=%wide.region_0.3_spmd.clone.sunk | while | flops 1513635840 | bytes 41485124 | solution.py:83
  21.1 5.3 collective-permute-done
  28.9 10.9 %conditional.6 = (f32[80,3072]{1,0:T(8,128)}) conditional(s32[]{:T(128)} %convert_element_type.157, () %tuple.100, (bf16[80,3072]{1,0:T(8,128)(2,1)}, bf16[3072,3072]{1,0:T(8,128)(2,1)}) %tuple.101), branch_computations={%region_1.1_spmd, %region_2.2_spmd} | conditional | flops 1509949440 | bytes 20348936 | solution.py:61
  28.9 10.9 %fusion.35 = f32[80,3072]{1,0:T(8,128)} fusion(bf16[80,3072]{1,0:T(8,128)(2,1)} %get-tuple-element.357, bf16[3072,3072]{1,0:T(8,128)(2,1)} %get-tuple-element.358), kind=kOutput, calls=%fused_computation.56 | convolution fusion | flops 1509949440 | bytes 20348928 | tf_op jit(solution)/shard_map/while/body/eval_jaxpr/cond/branch_1_fun/dot_general | solution.py:63
  51.4 4.7 collective-permute-done
  58.5 10.9 %conditional.6 = (f32[80,3072]{1,0:T(8,128)}) conditional(s32[]{:T(128)} %convert_element_type.157, () %tuple.100, (bf16[80,3072]{1,0:T(8,128)(2,1)}, bf16[3072,3072]{1,0:T(8,128)(2,1)}) %tuple.101), branch_computations={%region_1.1_spmd, %region_2.2_spmd} | conditional | flops 1509949440 | bytes 20348936 | solution.py:61
  58.5 10.9 %fusion.35 = f32[80,3072]{1,0:T(8,128)} fusion(bf16[80,3072]{1,0:T(8,128)(2,1)} %get-tuple-element.357, bf16[3072,3072]{1,0:T(8,128)(2,1)} %get-tuple-element.358), kind=kOutput, calls=%fused_computation.56 | convolution fusion | flops 1509949440 | bytes 20348928 | tf_op jit(solution)/shard_map/while/body/eval_jaxpr/cond/branch_1_fun/dot_general | solution.py:63
  74.9 5.0 collective-permute-start
  90.1 10.9 %conditional.6 = (f32[80,3072]{1,0:T(8,128)}) conditional(s32[]{:T(128)} %convert_element_type.157, () %tuple.100, (bf16[80,3072]{1,0:T(8,128)(2,1)}, bf16[3072,3072]{1,0:T(8,128)(2,1)}) %tuple.101), branch_computations={%region_1.1_spmd, %region_2.2_spmd} | conditional | flops 1509949440 | bytes 20348936 | solution.py:61
  90.1 10.9 %fusion.35 = f32[80,3072]{1,0:T(8,128)} fusion(bf16[80,3072]{1,0:T(8,128)(2,1)} %get-tuple-element.357, bf16[3072,3072]{1,0:T(8,128)(2,1)} %get-tuple-element.358), kind=kOutput, calls=%fused_computation.56 | convolution fusion | flops 1509949440 | bytes 20348928 | tf_op jit(solution)/shard_map/while/body/eval_jaxpr/cond/branch_1_fun/dot_general | solution.py:63
  106.5 5.1 collective-permute-start
  120.9 10.9 %conditional.6 = (f32[80,3072]{1,0:T(8,128)}) conditional(s32[]{:T(128)} %convert_element_type.157, () %tuple.100, (bf16[80,3072]{1,0:T(8,128)(2,1)}, bf16[3072,3072]{1,0:T(8,128)(2,1)}) %tuple.101), branch_computations={%region_1.1_spmd, %region_2.2_spmd} | conditional | flops 1509949440 | bytes 20348936 | solution.py:61
  120.9 10.9 %fusion.35 = f32[80,3072]{1,0:T(8,128)} fusion(bf16[80,3072]{1,0:T(8,128)(2,1)} %get-tuple-element.357, bf16[3072,3072]{1,0:T(8,128)(2,1)} %get-tuple-element.358), kind=kOutput, calls=%fused_computation.56 | convolution fusion | flops 1509949440 | bytes 20348928 | tf_op jit(solution)/shard_map/while/body/eval_jaxpr/cond/branch_1_fun/dot_general | solution.py:63
  137.3 5.1 collective-permute-start
  157.2 14.9 %collective-permute-start = (bf16[80,3072]{1,0:T(8,128)(2,1)}, bf16[80,3072]{1,0:T(8,128)(2,1)}, u32[]{:S(2)}, u32[]{:S(2)}) collective-permute-start(bf16[80,3072]{1,0:T(8,128)(2,1)} %broadcast_select_fusion.4), channel_id=1, source_target_pairs={{0,16},{16,32},{32,48},{48,64},{64,80},{80,96},{96,112},{1,17},{17... | collective-permute-start | bytes 1474568 | tf_op jit(solution)/shard_map/while/body/eval_jaxpr/ppermute | solution.py:21
  186.3 4.7 collective-permute-start
  205.2 13.9 %collective-permute-start = (bf16[80,3072]{1,0:T(8,128)(2,1)}, bf16[80,3072]{1,0:T(8,128)(2,1)}, u32[]{:S(2)}, u32[]{:S(2)}) collective-permute-start(bf16[80,3072]{1,0:T(8,128)(2,1)} %broadcast_select_fusion.4), channel_id=1, source_target_pairs={{0,16},{16,32},{32,48},{48,64},{64,80},{80,96},{96,112},{1,17},{17... | collective-permute-start | bytes 1474568 | tf_op jit(solution)/shard_map/while/body/eval_jaxpr/ppermute | solution.py:21
  233.3 4.7 collective-permute-start
  252.3 16.4 %collective-permute-start = (bf16[80,3072]{1,0:T(8,128)(2,1)}, bf16[80,3072]{1,0:T(8,128)(2,1)}, u32[]{:S(2)}, u32[]{:S(2)}) collective-permute-start(bf16[80,3072]{1,0:T(8,128)(2,1)} %broadcast_select_fusion.4), channel_id=1, source_target_pairs={{0,16},{16,32},{32,48},{48,64},{64,80},{80,96},{96,112},{1,17},{17... | collective-permute-start | bytes 1474568 | tf_op jit(solution)/shard_map/while/body/eval_jaxpr/ppermute | solution.py:21
  282.9 6.9 collective-permute-start
  305.3 5.5 reshape_reshape.6
  310.8 6.8 multiply_convert_fusion.1
  319.5 379.2 %while.38 = (s32[]{:T(128)}, bf16[80,3072]{1,0:T(8,128)(2,1)}, bf16[4,80,3072]{2,1,0:T(8,128)(2,1)}, pred[]{:T(512)}, s32[]{:T(128)}, /*index=5*/bf16[4,80,3072]...) while((s32[]{:T(128)}, bf16[80,3072]{1,0:T(8,128)(2,1)}, ...), condition=%wide.region_7.8_spmd.clone, body=%wide.region_4.7_spmd.clone.sunk | while | flops 1516830720 | bytes 30181076 | solution.py:115
  322.7 20.0 %collective-permute-done.1 = bf16[80,3072]{1,0:T(8,128)(2,1)} collective-permute-done((bf16[80,3072]{1,0:T(8,128)(2,1)}, bf16[80,3072]{1,0:T(8,128)(2,1)}, u32[]{:S(2)}, u32[]{:S(2)}) %collective-permute-start.1) | collective-permute-done | bytes 491552 | tf_op jit(solution)/shard_map/while/body/eval_jaxpr/ppermute | solution.py:21
  353.6 10.0 %collective-permute-done.1 = bf16[80,3072]{1,0:T(8,128)(2,1)} collective-permute-done((bf16[80,3072]{1,0:T(8,128)(2,1)}, bf16[80,3072]{1,0:T(8,128)(2,1)}, u32[]{:S(2)}, u32[]{:S(2)}) %collective-permute-start.1) | collective-permute-done | bytes 491552 | tf_op jit(solution)/shard_map/while/body/eval_jaxpr/ppermute | solution.py:21
  374.6 13.8 %collective-permute-done.1 = bf16[80,3072]{1,0:T(8,128)(2,1)} collective-permute-done((bf16[80,3072]{1,0:T(8,128)(2,1)}, bf16[80,3072]{1,0:T(8,128)(2,1)}, u32[]{:S(2)}, u32[]{:S(2)}) %collective-permute-start.1) | collective-permute-done | bytes 491552 | tf_op jit(solution)/shard_map/while/body/eval_jaxpr/ppermute | solution.py:21
  399.4 10.1 %collective-permute-done.1 = bf16[80,3072]{1,0:T(8,128)(2,1)} collective-permute-done((bf16[80,3072]{1,0:T(8,128)(2,1)}, bf16[80,3072]{1,0:T(8,128)(2,1)}, u32[]{:S(2)}, u32[]{:S(2)}) %collective-permute-start.1) | collective-permute-done | bytes 491552 | tf_op jit(solution)/shard_map/while/body/eval_jaxpr/ppermute | solution.py:21
  420.5 13.8 %collective-permute-done.1 = bf16[80,3072]{1,0:T(8,128)(2,1)} collective-permute-done((bf16[80,3072]{1,0:T(8,128)(2,1)}, bf16[80,3072]{1,0:T(8,128)(2,1)}, u32[]{:S(2)}, u32[]{:S(2)}) %collective-permute-start.1) | collective-permute-done | bytes 491552 | tf_op jit(solution)/shard_map/while/body/eval_jaxpr/ppermute | solution.py:21
  445.2 9.8 %collective-permute-done.1 = bf16[80,3072]{1,0:T(8,128)(2,1)} collective-permute-done((bf16[80,3072]{1,0:T(8,128)(2,1)}, bf16[80,3072]{1,0:T(8,128)(2,1)}, u32[]{:S(2)}, u32[]{:S(2)}) %collective-permute-start.1) | collective-permute-done | bytes 491552 | tf_op jit(solution)/shard_map/while/body/eval_jaxpr/ppermute | solution.py:21
  466.0 13.6 %collective-permute-done.1 = bf16[80,3072]{1,0:T(8,128)(2,1)} collective-permute-done((bf16[80,3072]{1,0:T(8,128)(2,1)}, bf16[80,3072]{1,0:T(8,128)(2,1)}, u32[]{:S(2)}, u32[]{:S(2)}) %collective-permute-start.1) | collective-permute-done | bytes 491552 | tf_op jit(solution)/shard_map/while/body/eval_jaxpr/ppermute | solution.py:21
  490.6 90.5 %collective-permute-done.1 = bf16[80,3072]{1,0:T(8,128)(2,1)} collective-permute-done((bf16[80,3072]{1,0:T(8,128)(2,1)}, bf16[80,3072]{1,0:T(8,128)(2,1)}, u32[]{:S(2)}, u32[]{:S(2)}) %collective-permute-start.1) | collective-permute-done | bytes 491552 | tf_op jit(solution)/shard_map/while/body/eval_jaxpr/ppermute | solution.py:21
  584.3 13.3 %conditional.7 = (f32[80,3072]{1,0:T(8,128)}) conditional(s32[]{:T(128)} %convert_element_type.160, () %tuple.104, (bf16[80,3072]{1,0:T(8,128)(2,1)}, bf16[3072,3072]{1,0:T(8,128)(2,1)}) %tuple.105), branch_computations={%region_5.5_spmd, %region_6.6_spmd} | conditional | flops 1509949440 | bytes 20348936 | solution.py:99
  584.3 13.3 %fusion.36 = f32[80,3072]{1,0:T(8,128)} fusion(bf16[80,3072]{1,0:T(8,128)(2,1)} %get-tuple-element.368, bf16[3072,3072]{1,0:T(8,128)(2,1)} %get-tuple-element.369), kind=kOutput, calls=%fused_computation.57 | convolution fusion | flops 1509949440 | bytes 20348928 | tf_op jit(solution)/shard_map/while/body/eval_jaxpr/cond/branch_1_fun/dot_general | solution.py:101
  604.3 9.7 collective-permute-done.1
  617.3 13.3 %conditional.7 = (f32[80,3072]{1,0:T(8,128)}) conditional(s32[]{:T(128)} %convert_element_type.160, () %tuple.104, (bf16[80,3072]{1,0:T(8,128)(2,1)}, bf16[3072,3072]{1,0:T(8,128)(2,1)}) %tuple.105), branch_computations={%region_5.5_spmd, %region_6.6_spmd} | conditional | flops 1509949440 | bytes 20348936 | solution.py:99
  617.3 13.3 %fusion.36 = f32[80,3072]{1,0:T(8,128)} fusion(bf16[80,3072]{1,0:T(8,128)(2,1)} %get-tuple-element.368, bf16[3072,3072]{1,0:T(8,128)(2,1)} %get-tuple-element.369), kind=kOutput, calls=%fused_computation.57 | convolution fusion | flops 1509949440 | bytes 20348928 | tf_op jit(solution)/shard_map/while/body/eval_jaxpr/cond/branch_1_fun/dot_general | solution.py:101
  637.3 9.5 collective-permute-done.1
  650.2 13.3 %conditional.7 = (f32[80,3072]{1,0:T(8,128)}) conditional(s32[]{:T(128)} %convert_element_type.160, () %tuple.104, (bf16[80,3072]{1,0:T(8,128)(2,1)}, bf16[3072,3072]{1,0:T(8,128)(2,1)}) %tuple.105), branch_computations={%region_5.5_spmd, %region_6.6_spmd} | conditional | flops 1509949440 | bytes 20348936 | solution.py:99
  650.2 13.3 %fusion.36 = f32[80,3072]{1,0:T(8,128)} fusion(bf16[80,3072]{1,0:T(8,128)(2,1)} %get-tuple-element.368, bf16[3072,3072]{1,0:T(8,128)(2,1)} %get-tuple-element.369), kind=kOutput, calls=%fused_computation.57 | convolution fusion | flops 1509949440 | bytes 20348928 | tf_op jit(solution)/shard_map/while/body/eval_jaxpr/cond/branch_1_fun/dot_general | solution.py:101
  670.1 9.5 collective-permute-done.1
  682.9 13.3 %conditional.7 = (f32[80,3072]{1,0:T(8,128)}) conditional(s32[]{:T(128)} %convert_element_type.160, () %tuple.104, (bf16[80,3072]{1,0:T(8,128)(2,1)}, bf16[3072,3072]{1,0:T(8,128)(2,1)}) %tuple.105), branch_computations={%region_5.5_spmd, %region_6.6_spmd} | conditional | flops 1509949440 | bytes 20348936 | solution.py:99
  682.9 13.3 %fusion.36 = f32[80,3072]{1,0:T(8,128)} fusion(bf16[80,3072]{1,0:T(8,128)(2,1)} %get-tuple-element.368, bf16[3072,3072]{1,0:T(8,128)(2,1)} %get-tuple-element.369), kind=kOutput, calls=%fused_computation.57 | convolution fusion | flops 1509949440 | bytes 20348928 | tf_op jit(solution)/shard_map/while/body/eval_jaxpr/cond/branch_1_fun/dot_general | solution.py:101
  698.7 5.5 reshape_reshape.7
  704.2 6.9 multiply_convert_fusion
  711.4 16.0 %bitcast_convert_fusion = bf16[3072,3072]{1,0:T(8,128)(2,1)} fusion(bf16[4,80,3072]{2,1,0:T(8,128)(2,1)} %get-tuple-element.386, bf16[4,80,3072]{2,1,0:T(8,128)(2,1)} %get-tuple-element.388), kind=kOutput, calls=%fused_computation.37 | convolution fusion | flops 6049234944 | bytes 22806528 | tf_op jit(solution)/shard_map/dot_general | solution.py:129
  729.1 66.8 %reduce-scatter.8.cloned.1.call-done = bf16[1,192,192]{2,1,0:T(8,128)(2,1)} async-done(((bf16[16,192,192]{2,1,0:T(8,128)(2,1)}), bf16[1,192,192]{2,1,0:T(8,128)(2,1)}) %reduce-scatter.8.cloned.1.call-update) | async-done | bytes 73744 | tf_op jit(solution)/shard_map/reduce_scatter | solution.py:122
  797.5 158.8 %reduce-scatter.4.cloned.1.call-done = bf16[192,3072]{1,0:T(8,128)(2,1)} async-done(((bf16[3072,3072]{1,0:T(8,128)(2,1)}), bf16[192,3072]{1,0:T(8,128)(2,1)}) %reduce-scatter.4.cloned.1.call-update) | async-done | bytes 1179664 | tf_op jit(solution)/shard_map/reduce_scatter | solution.py:128
  961.7 7.2 multiply_convert_fusion.2
  (241 shorter events, 310.7 us)
Async XLA Ops:
  7.2 954.6 %copy-start = (f32[1,16,192,192]{3,2,1,0:T(8,128)S(1)}, f32[1,16,192,192]{3,2,1,0:T(8,128)}, u32[]{:S(2)}) copy-start(f32[1,16,192,192]{3,2,1,0:T(8,128)} %param.19) | copy-start | bytes 7077892
  7.2 720.2 %reduce-scatter.6.cloned.1.call-start = ((), (), s32[]{:S(2)}) async-start(), calls=%async_computation.4 | async-start | bytes 1671168 | tf_op jit(solution)/shard_map/reduce_scatter | solution.py:119
  12.8 13.7 %collective-permute-start = (bf16[80,3072]{1,0:T(8,128)(2,1)}, bf16[80,3072]{1,0:T(8,128)(2,1)}, u32[]{:S(2)}, u32[]{:S(2)}) collective-permute-start(bf16[80,3072]{1,0:T(8,128)(2,1)} %broadcast_select_fusion.4), channel_id=1, source_target_pairs={{0,16},{16,32},{32,48},{48,64},{64,80},{80,96},{96,112},{1,17},{17... | collective-permute-start | bytes 1474568 | tf_op jit(solution)/shard_map/while/body/eval_jaxpr/ppermute | solution.py:21
  39.7 2.6 copy-start.1
  39.7 2.6 copy-start.2
  45.3 10.8 %collective-permute-start = (bf16[80,3072]{1,0:T(8,128)(2,1)}, bf16[80,3072]{1,0:T(8,128)(2,1)}, u32[]{:S(2)}, u32[]{:S(2)}) collective-permute-start(bf16[80,3072]{1,0:T(8,128)(2,1)} %broadcast_select_fusion.4), channel_id=1, source_target_pairs={{0,16},{16,32},{32,48},{48,64},{64,80},{80,96},{96,112},{1,17},{17... | collective-permute-start | bytes 1474568 | tf_op jit(solution)/shard_map/while/body/eval_jaxpr/ppermute | solution.py:21
  69.3 2.6 copy-start.1
  69.3 2.6 copy-start.2
  74.9 12.8 %collective-permute-start = (bf16[80,3072]{1,0:T(8,128)(2,1)}, bf16[80,3072]{1,0:T(8,128)(2,1)}, u32[]{:S(2)}, u32[]{:S(2)}) collective-permute-start(bf16[80,3072]{1,0:T(8,128)(2,1)} %broadcast_select_fusion.4), channel_id=1, source_target_pairs={{0,16},{16,32},{32,48},{48,64},{64,80},{80,96},{96,112},{1,17},{17... | collective-permute-start | bytes 1474568 | tf_op jit(solution)/shard_map/while/body/eval_jaxpr/ppermute | solution.py:21
  100.9 2.6 copy-start.1
  100.9 2.6 copy-start.2
  106.5 12.0 %collective-permute-start = (bf16[80,3072]{1,0:T(8,128)(2,1)}, bf16[80,3072]{1,0:T(8,128)(2,1)}, u32[]{:S(2)}, u32[]{:S(2)}) collective-permute-start(bf16[80,3072]{1,0:T(8,128)(2,1)} %broadcast_select_fusion.4), channel_id=1, source_target_pairs={{0,16},{16,32},{32,48},{48,64},{64,80},{80,96},{96,112},{1,17},{17... | collective-permute-start | bytes 1474568 | tf_op jit(solution)/shard_map/while/body/eval_jaxpr/ppermute | solution.py:21
  131.7 2.6 copy-start.1
  131.7 2.6 copy-start.2
  137.3 11.0 %collective-permute-start = (bf16[80,3072]{1,0:T(8,128)(2,1)}, bf16[80,3072]{1,0:T(8,128)(2,1)}, u32[]{:S(2)}, u32[]{:S(2)}) collective-permute-start(bf16[80,3072]{1,0:T(8,128)(2,1)} %broadcast_select_fusion.4), channel_id=1, source_target_pairs={{0,16},{16,32},{32,48},{48,64},{64,80},{80,96},{96,112},{1,17},{17... | collective-permute-start | bytes 1474568 | tf_op jit(solution)/shard_map/while/body/eval_jaxpr/ppermute | solution.py:21
  151.7 2.6 copy-start.1
  151.7 2.6 copy-start.2
  157.2 20.1 %collective-permute-start = (bf16[80,3072]{1,0:T(8,128)(2,1)}, bf16[80,3072]{1,0:T(8,128)(2,1)}, u32[]{:S(2)}, u32[]{:S(2)}) collective-permute-start(bf16[80,3072]{1,0:T(8,128)(2,1)} %broadcast_select_fusion.4), channel_id=1, source_target_pairs={{0,16},{16,32},{32,48},{48,64},{64,80},{80,96},{96,112},{1,17},{17... | collective-permute-start | bytes 1474568 | tf_op jit(solution)/shard_map/while/body/eval_jaxpr/ppermute | solution.py:21
  180.7 2.6 copy-start.1
  180.7 2.6 copy-start.2
  186.3 10.0 %collective-permute-start = (bf16[80,3072]{1,0:T(8,128)(2,1)}, bf16[80,3072]{1,0:T(8,128)(2,1)}, u32[]{:S(2)}, u32[]{:S(2)}) collective-permute-start(bf16[80,3072]{1,0:T(8,128)(2,1)} %broadcast_select_fusion.4), channel_id=1, source_target_pairs={{0,16},{16,32},{32,48},{48,64},{64,80},{80,96},{96,112},{1,17},{17... | collective-permute-start | bytes 1474568 | tf_op jit(solution)/shard_map/while/body/eval_jaxpr/ppermute | solution.py:21
  199.7 2.6 copy-start.1
  199.7 2.6 copy-start.2
  205.2 19.2 %collective-permute-start = (bf16[80,3072]{1,0:T(8,128)(2,1)}, bf16[80,3072]{1,0:T(8,128)(2,1)}, u32[]{:S(2)}, u32[]{:S(2)}) collective-permute-start(bf16[80,3072]{1,0:T(8,128)(2,1)} %broadcast_select_fusion.4), channel_id=1, source_target_pairs={{0,16},{16,32},{32,48},{48,64},{64,80},{80,96},{96,112},{1,17},{17... | collective-permute-start | bytes 1474568 | tf_op jit(solution)/shard_map/while/body/eval_jaxpr/ppermute | solution.py:21
  227.8 2.6 copy-start.1
  227.8 2.6 copy-start.2
  233.3 10.0 %collective-permute-start = (bf16[80,3072]{1,0:T(8,128)(2,1)}, bf16[80,3072]{1,0:T(8,128)(2,1)}, u32[]{:S(2)}, u32[]{:S(2)}) collective-permute-start(bf16[80,3072]{1,0:T(8,128)(2,1)} %broadcast_select_fusion.4), channel_id=1, source_target_pairs={{0,16},{16,32},{32,48},{48,64},{64,80},{80,96},{96,112},{1,17},{17... | collective-permute-start | bytes 1474568 | tf_op jit(solution)/shard_map/while/body/eval_jaxpr/ppermute | solution.py:21
  246.7 2.6 copy-start.1
  246.7 2.6 copy-start.2
  252.3 21.7 %collective-permute-start = (bf16[80,3072]{1,0:T(8,128)(2,1)}, bf16[80,3072]{1,0:T(8,128)(2,1)}, u32[]{:S(2)}, u32[]{:S(2)}) collective-permute-start(bf16[80,3072]{1,0:T(8,128)(2,1)} %broadcast_select_fusion.4), channel_id=1, source_target_pairs={{0,16},{16,32},{32,48},{48,64},{64,80},{80,96},{96,112},{1,17},{17... | collective-permute-start | bytes 1474568 | tf_op jit(solution)/shard_map/while/body/eval_jaxpr/ppermute | solution.py:21
  277.4 2.6 copy-start.2
  282.9 12.2 %collective-permute-start = (bf16[80,3072]{1,0:T(8,128)(2,1)}, bf16[80,3072]{1,0:T(8,128)(2,1)}, u32[]{:S(2)}, u32[]{:S(2)}) collective-permute-start(bf16[80,3072]{1,0:T(8,128)(2,1)} %broadcast_select_fusion.4), channel_id=1, source_target_pairs={{0,16},{16,32},{32,48},{48,64},{64,80},{80,96},{96,112},{1,17},{17... | collective-permute-start | bytes 1474568 | tf_op jit(solution)/shard_map/while/body/eval_jaxpr/ppermute | solution.py:21
  298.5 2.6 copy-start.2
  310.8 7.1 copy-start.4
  317.6 478.3 %reduce-scatter.8.cloned.1.call-start = ((), (), s32[]{:S(2)}) async-start(), calls=%async_computation.5 | async-start | bytes 1671168 | tf_op jit(solution)/shard_map/reduce_scatter | solution.py:122
  320.3 22.4 %collective-permute-start.1 = (bf16[80,3072]{1,0:T(8,128)(2,1)}, bf16[80,3072]{1,0:T(8,128)(2,1)}, u32[]{:S(2)}, u32[]{:S(2)}) collective-permute-start(bf16[80,3072]{1,0:T(8,128)(2,1)} %broadcast_select_fusion.5), channel_id=1, source_target_pairs={{16,0},{32,16},{48,32},{64,48},{80,64},{96,80},{112,96},{17,1},{33... | collective-permute-start | bytes 1474568 | tf_op jit(solution)/shard_map/while/body/eval_jaxpr/ppermute | solution.py:21
  351.2 12.4 %collective-permute-start.1 = (bf16[80,3072]{1,0:T(8,128)(2,1)}, bf16[80,3072]{1,0:T(8,128)(2,1)}, u32[]{:S(2)}, u32[]{:S(2)}) collective-permute-start(bf16[80,3072]{1,0:T(8,128)(2,1)} %broadcast_select_fusion.5), channel_id=1, source_target_pairs={{16,0},{32,16},{48,32},{64,48},{80,64},{96,80},{112,96},{17,1},{33... | collective-permute-start | bytes 1474568 | tf_op jit(solution)/shard_map/while/body/eval_jaxpr/ppermute | solution.py:21
  372.2 16.1 %collective-permute-start.1 = (bf16[80,3072]{1,0:T(8,128)(2,1)}, bf16[80,3072]{1,0:T(8,128)(2,1)}, u32[]{:S(2)}, u32[]{:S(2)}) collective-permute-start(bf16[80,3072]{1,0:T(8,128)(2,1)} %broadcast_select_fusion.5), channel_id=1, source_target_pairs={{16,0},{32,16},{48,32},{64,48},{80,64},{96,80},{112,96},{17,1},{33... | collective-permute-start | bytes 1474568 | tf_op jit(solution)/shard_map/while/body/eval_jaxpr/ppermute | solution.py:21
  397.0 12.5 %collective-permute-start.1 = (bf16[80,3072]{1,0:T(8,128)(2,1)}, bf16[80,3072]{1,0:T(8,128)(2,1)}, u32[]{:S(2)}, u32[]{:S(2)}) collective-permute-start(bf16[80,3072]{1,0:T(8,128)(2,1)} %broadcast_select_fusion.5), channel_id=1, source_target_pairs={{16,0},{32,16},{48,32},{64,48},{80,64},{96,80},{112,96},{17,1},{33... | collective-permute-start | bytes 1474568 | tf_op jit(solution)/shard_map/while/body/eval_jaxpr/ppermute | solution.py:21
  418.1 16.2 %collective-permute-start.1 = (bf16[80,3072]{1,0:T(8,128)(2,1)}, bf16[80,3072]{1,0:T(8,128)(2,1)}, u32[]{:S(2)}, u32[]{:S(2)}) collective-permute-start(bf16[80,3072]{1,0:T(8,128)(2,1)} %broadcast_select_fusion.5), channel_id=1, source_target_pairs={{16,0},{32,16},{48,32},{64,48},{80,64},{96,80},{112,96},{17,1},{33... | collective-permute-start | bytes 1474568 | tf_op jit(solution)/shard_map/while/body/eval_jaxpr/ppermute | solution.py:21
  442.8 12.2 %collective-permute-start.1 = (bf16[80,3072]{1,0:T(8,128)(2,1)}, bf16[80,3072]{1,0:T(8,128)(2,1)}, u32[]{:S(2)}, u32[]{:S(2)}) collective-permute-start(bf16[80,3072]{1,0:T(8,128)(2,1)} %broadcast_select_fusion.5), channel_id=1, source_target_pairs={{16,0},{32,16},{48,32},{64,48},{80,64},{96,80},{112,96},{17,1},{33... | collective-permute-start | bytes 1474568 | tf_op jit(solution)/shard_map/while/body/eval_jaxpr/ppermute | solution.py:21
  463.6 16.0 %collective-permute-start.1 = (bf16[80,3072]{1,0:T(8,128)(2,1)}, bf16[80,3072]{1,0:T(8,128)(2,1)}, u32[]{:S(2)}, u32[]{:S(2)}) collective-permute-start(bf16[80,3072]{1,0:T(8,128)(2,1)} %broadcast_select_fusion.5), channel_id=1, source_target_pairs={{16,0},{32,16},{48,32},{64,48},{80,64},{96,80},{112,96},{17,1},{33... | collective-permute-start | bytes 1474568 | tf_op jit(solution)/shard_map/while/body/eval_jaxpr/ppermute | solution.py:21
  488.2 92.9 %collective-permute-start.1 = (bf16[80,3072]{1,0:T(8,128)(2,1)}, bf16[80,3072]{1,0:T(8,128)(2,1)}, u32[]{:S(2)}, u32[]{:S(2)}) collective-permute-start(bf16[80,3072]{1,0:T(8,128)(2,1)} %broadcast_select_fusion.5), channel_id=1, source_target_pairs={{16,0},{32,16},{48,32},{64,48},{80,64},{96,80},{112,96},{17,1},{33... | collective-permute-start | bytes 1474568 | tf_op jit(solution)/shard_map/while/body/eval_jaxpr/ppermute | solution.py:21
  601.9 12.1 %collective-permute-start.1 = (bf16[80,3072]{1,0:T(8,128)(2,1)}, bf16[80,3072]{1,0:T(8,128)(2,1)}, u32[]{:S(2)}, u32[]{:S(2)}) collective-permute-start(bf16[80,3072]{1,0:T(8,128)(2,1)} %broadcast_select_fusion.5), channel_id=1, source_target_pairs={{16,0},{32,16},{48,32},{64,48},{80,64},{96,80},{112,96},{17,1},{33... | collective-permute-start | bytes 1474568 | tf_op jit(solution)/shard_map/while/body/eval_jaxpr/ppermute | solution.py:21
  634.9 11.9 %collective-permute-start.1 = (bf16[80,3072]{1,0:T(8,128)(2,1)}, bf16[80,3072]{1,0:T(8,128)(2,1)}, u32[]{:S(2)}, u32[]{:S(2)}) collective-permute-start(bf16[80,3072]{1,0:T(8,128)(2,1)} %broadcast_select_fusion.5), channel_id=1, source_target_pairs={{16,0},{32,16},{48,32},{64,48},{80,64},{96,80},{112,96},{17,1},{33... | collective-permute-start | bytes 1474568 | tf_op jit(solution)/shard_map/while/body/eval_jaxpr/ppermute | solution.py:21
  667.7 11.9 %collective-permute-start.1 = (bf16[80,3072]{1,0:T(8,128)(2,1)}, bf16[80,3072]{1,0:T(8,128)(2,1)}, u32[]{:S(2)}, u32[]{:S(2)}) collective-permute-start(bf16[80,3072]{1,0:T(8,128)(2,1)} %broadcast_select_fusion.5), channel_id=1, source_target_pairs={{16,0},{32,16},{48,32},{64,48},{80,64},{96,80},{112,96},{17,1},{33... | collective-permute-start | bytes 1474568 | tf_op jit(solution)/shard_map/while/body/eval_jaxpr/ppermute | solution.py:21
  711.1 245.2 %reduce-scatter.4.cloned.1.call-start = ((), (), s32[]{:S(2)}) async-start(), calls=%async_computation.3 | async-start | bytes 20054016 | tf_op jit(solution)/shard_map/reduce_scatter | solution.py:128
  727.4 231.5 %copy-start.3 = (f32[1,1,192,192]{3,2,1,0:T(8,128)S(1)}, f32[1,1,192,192]{3,2,1,0:T(8,128)}, u32[]{:S(2)}) copy-start(f32[1,1,192,192]{3,2,1,0:T(8,128)} %param.18) | copy-start | bytes 442372
  (2 other events, 5.3 us)
Sparse Core Ops, SparseCore 0:
  317.7 118.0 reduce-scatter.5
  711.2 84.6 reduce-scatter.7
  800.3 155.9 reduce-scatter.3
where the time goes:
time: 986 us; the launch traced here: 978 us
  waiting for transfers between devices  462 us (47%)
  other arithmetic  175 us (18%)
  matrix products  136 us (14%)
  starting transfers between devices  97.7 us (10%)
  local copies, waits for them, and re-layouts  92.4 us (9%)
  between operations  13.8 us (1%)
    ppermute x22, waiting for transfers between devices, from_behind(): return lax.ppermute(x, axis, pairs)  236 us
    reduce_scatter x1, waiting for transfers between devices, shards(): lax.psum_scatter(lax.dot_general(left, scaled_flat, (((0,), (0,)), ((), (...  159 us
    ppermute x22, starting transfers between devices, from_behind(): return lax.ppermute(x, axis, pairs)  97.2 us
    reduce_scatter x1, waiting for transfers between devices, shards(): lax.psum_scatter(gram_out.astype(jnp.bfloat16), 'dp', scatter_dimension=0...  66.8 us
    dot_general x4, matrix products, backward_tick(): lax.dot_general(v, matrix, (((1,), (1,)), ((), ())), preferred_element_ty...  53.2 us
    dot_general x4, matrix products, forward_tick(): jnp.dot(v, matrix, preferred_element_type=jnp.float32)  43.4 us
    while x22, other arithmetic  38.5 us
    dynamic_update_slice x11, other arithmetic, backward_tick(): lax.dynamic_update_index_in_dim(stored_scaled, jnp.where(valid, scaled, o...  36.1 us
  transfers between devices with their start and end apart: 25, of which 24 were waited for; matrix products, arithmetic and copies ran while one was open for 24% of the time, Pallas kernels for 0%

commit v1 on v0

v1 whole, which is shorter than its diff:
```python
import functools

import jax
import jax.numpy as jnp
from jax import lax
from jax.experimental import pallas as pl
from jax.experimental.pallas import tpu as pltpu
from jax.sharding import PartitionSpec as P

D = 3072
HALF = D // 2
BLOCK = 192
MICRO = 4
ROWS = 80
TOK_DEV = 320
LIVE = 240
NBLK = 16
PAIR = 2 * LIVE
CHUNK = 48
CHUNKS = PAIR // CHUNK
PIECES = 3
WIDTH = HALF // PIECES

C_ZERO = 0.7978845608028654
C_ONE = 0.044715
MESH = pl.DeviceIdType.MESH


def activate(value):
    return 0.5 * value * (1.0 + jnp.tanh(C_ZERO * (value + C_ONE * value * value * value)))


def slope(value):
    hyper = jnp.tanh(C_ZERO * (value + C_ONE * value * value * value))
    return 0.5 * (1.0 + hyper) + 0.5 * value * (1.0 - hyper * hyper) * C_ZERO * (
        1.0 + 3.0 * C_ONE * value * value
    )


def block_gram(rows_data, total):
    blocks = rows_data.reshape(rows_data.shape[0], NBLK, BLOCK)
    return jnp.einsum("tkb,tkc->kbc", blocks, blocks, preferred_element_type=jnp.float32) / total


def mm(a, b):
    return jnp.dot(a, b, preferred_element_type=jnp.float32)


def pipeline(
    stages,
    source,
    weight,
    x_out,
    s_out,
    x_buf,
    s_buf,
    g_buf,
    slopes,
    f_send,
    b_send,
    w_fwd,
    w_bwd,
    w_raw,
    acc,
    load_sem,
    init_send,
    init_recv,
    f_send_sem,
    f_recv_sem,
    b_send_sem,
    b_recv_sem,
    xs_send_sem,
    xs_recv_sem,
    ss_send_sem,
    ss_recv_sem,
):
    stage = lax.axis_index("section")
    rank = lax.axis_index("dp")
    core = lax.rem(rank, 2)
    sibling = {"dp": rank + 1 - 2 * core}
    last = stages - 1
    following = {"section": jnp.minimum(stage + 1, last)}
    previous = {"section": jnp.maximum(stage - 1, 0)}
    own_cols = pl.ds(pl.multiple_of(core * HALF, HALF), HALF)
    sib_cols = pl.ds(pl.multiple_of((1 - core) * HALF, HALF), HALF)

    loads = (
        pltpu.make_async_copy(weight.at[own_cols, own_cols], w_fwd.at[0], load_sem.at[0]),
        pltpu.make_async_copy(weight.at[sib_cols, own_cols], w_fwd.at[1], load_sem.at[1]),
        pltpu.make_async_copy(weight.at[own_cols, sib_cols], w_raw, load_sem.at[2]),
    )
    for load in loads:
        load.start()

    barrier = pltpu.get_barrier_semaphore()
    pl.semaphore_signal(barrier, inc=1, device_id=sibling, device_id_type=MESH)

    @pl.when(stage > 0)
    def _():
        pl.semaphore_signal(barrier, inc=1, device_id=previous, device_id_type=MESH)

    @pl.when(stage < last)
    def _():
        pl.semaphore_signal(barrier, inc=1, device_id=following, device_id_type=MESH)

    pl.semaphore_wait(
        barrier, 1 + (stage > 0).astype(jnp.int32) + (stage < last).astype(jnp.int32)
    )

    mine = pl.ds(pl.multiple_of(core * LIVE, 16), LIVE)

    @pl.when(stage == 0)
    def _():
        moves = (
            pltpu.make_async_copy(source.at[core], x_buf.at[0, mine], load_sem.at[3]),
            pltpu.make_async_copy(source.at[1 - core], x_buf.at[1, mine], load_sem.at[4]),
            pltpu.make_async_remote_copy(
                source.at[1 - core], x_buf.at[0, mine], init_send.at[0], init_recv.at[0],
                device_id=sibling, device_id_type=MESH,
            ),
            pltpu.make_async_remote_copy(
                source.at[core], x_buf.at[1, mine], init_send.at[1], init_recv.at[1],
                device_id=sibling, device_id_type=MESH,
            ),
        )
        for move in moves:
            move.start()
        for move in moves:
            move.wait()

    @pl.when(stage == last)
    def _():
        moves = (
            pltpu.make_async_copy(source.at[core], g_buf.at[mine], load_sem.at[3]),
            pltpu.make_async_remote_copy(
                source.at[1 - core], g_buf.at[mine], init_send.at[0], init_recv.at[0],
                device_id=sibling, device_id_type=MESH,
            ),
        )
        for move in moves:
            move.start()
        for move in moves:
            move.wait()

    for load in loads:
        load.wait()

    def rows_of(k):
        return pl.ds(pl.multiple_of(k * CHUNK, 16), CHUNK)

    def cols_of(p):
        return pl.ds(p * WIDTH, WIDTH)

    def f_copy(k, p):
        return pltpu.make_async_remote_copy(
            f_send.at[rows_of(k), cols_of(p)], x_buf.at[0, rows_of(k), cols_of(p)],
            f_send_sem.at[k, p], f_recv_sem.at[k, p], device_id=following, device_id_type=MESH,
        )

    def b_copy(k, p):
        return pltpu.make_async_remote_copy(
            b_send.at[rows_of(k), cols_of(p)], g_buf.at[rows_of(k), cols_of(p)],
            b_send_sem.at[k, p], b_recv_sem.at[k, p], device_id=previous, device_id_type=MESH,
        )

    def x_copy(k, p):
        return pltpu.make_async_remote_copy(
            x_buf.at[0, rows_of(k), cols_of(p)], x_buf.at[1, rows_of(k), cols_of(p)],
            xs_send_sem.at[k, p], xs_recv_sem.at[k, p], device_id=sibling, device_id_type=MESH,
        )

    def s_copy(k, p):
        return pltpu.make_async_remote_copy(
            s_buf.at[0, rows_of(k), cols_of(p)], s_buf.at[1, rows_of(k), cols_of(p)],
            ss_send_sem.at[k, p], ss_recv_sem.at[k, p], device_id=sibling, device_id_type=MESH,
        )

    def forward(k):
        rows = rows_of(k)
        for p in range(PIECES):
            cols = cols_of(p)

            @pl.when(stage > 0)
            def _():
                f_copy(k, p).wait_recv()
                x_copy(k, p).start()

            term = mm(x_buf[0, rows, cols], w_fwd[0, cols, :])
            acc[...] = term if p == 0 else acc[...] + term
        for p in range(PIECES):

            @pl.when(stage > 0)
            def _():
                x_copy(k, p).wait_recv()

            cols = cols_of(p)
            if p < PIECES - 1:
                acc[...] += mm(x_buf[1, rows, cols], w_fwd[1, cols, :])
        end = cols_of(PIECES - 1)
        for p in range(PIECES):
            cols = cols_of(p)
            pre = acc[:, cols] + mm(x_buf[1, rows, end], w_fwd[1, end, cols])
            slopes[rows, cols] = pre

            @pl.when(stage < last)
            def _():
                f_send[rows, cols] = (
                    x_buf[0, rows, cols].astype(jnp.float32) + activate(pre)
                ).astype(jnp.bfloat16)
                f_copy(k, p).start()

        slopes[rows, :] = slope(slopes[rows, :])

    def backward(k):
        rows = rows_of(k)
        for p in range(PIECES):
            cols = cols_of(p)

            @pl.when(stage < last)
            def _():
                b_copy(k, p).wait_recv()

            s_buf[0, rows, cols] = (
                g_buf[rows, cols].astype(jnp.float32) * slopes[rows, cols]
            ).astype(jnp.bfloat16)
            s_copy(k, p).start()

            @pl.when(stage > 0)
            def _():
                term = mm(s_buf[0, rows, cols], w_bwd[0, cols, :])
                acc[...] = term if p == 0 else acc[...] + term

        for p in range(PIECES):
            s_copy(k, p).wait_recv()
            cols = cols_of(p)
            if p < PIECES - 1:

                @pl.when(stage > 0)
                def _():
                    acc[...] += mm(s_buf[1, rows, cols], w_bwd[1, cols, :])

        @pl.when(stage > 0)
        def _():
            end = cols_of(PIECES - 1)
            for p in range(PIECES):
                cols = cols_of(p)
                back = acc[:, cols] + mm(s_buf[1, rows, end], w_bwd[1, end, cols])
                b_send[rows, cols] = (
                    g_buf[rows, cols].astype(jnp.float32) + back
                ).astype(jnp.bfloat16)
                b_copy(k, p).start()

    turn_at = jnp.where(2 * stage + CHUNKS > 2 * last, 0, stage + CHUNKS)
    tile = 256

    def turn():
        def step(i, carry):
            at = pl.ds(pl.multiple_of(i * tile, tile), tile)
            for j in range(HALF // tile):
                to = pl.ds(j * tile, tile)
                w_bwd[0, to, at] = w_fwd[0, at, to].T
                w_bwd[1, to, at] = w_raw[at, to].T
            return carry

        lax.fori_loop(0, HALF // tile, step, 0)

    def slot(t, carry):
        @pl.when((t == turn_at) & (stage > 0))
        def _():
            turn()

        kf = t - stage

        @pl.when((kf >= 0) & (kf < CHUNKS))
        def _():
            forward(kf)

        kb = t - (2 * last - stage)

        @pl.when((kb >= 0) & (kb < CHUNKS))
        def _():
            backward(kb)

        return carry

    lax.fori_loop(0, 2 * last + CHUNKS, slot, 0)

    outs = (
        pltpu.make_async_copy(x_buf.at[0], x_out.at[core], load_sem.at[0]),
        pltpu.make_async_copy(x_buf.at[1], x_out.at[1 - core], load_sem.at[1]),
        pltpu.make_async_copy(s_buf.at[0], s_out.at[core], load_sem.at[2]),
        pltpu.make_async_copy(s_buf.at[1], s_out.at[1 - core], load_sem.at[3]),
    )
    for out in outs:
        out.start()

    def drain(k, carry):
        for p in range(PIECES):

            @pl.when(stage < last)
            def _():
                f_copy(k, p).wait_send()

            @pl.when(stage > 0)
            def _():
                x_copy(k, p).wait_send()
                b_copy(k, p).wait_send()

            s_copy(k, p).wait_send()
        return carry

    lax.fori_loop(0, CHUNKS, drain, 0)
    for out in outs:
        out.wait()


def run_pipeline(source, matrix):
    dma = pltpu.SemaphoreType.DMA
    any_space = pl.BlockSpec(memory_space=pl.ANY)
    pieces = (CHUNKS, PIECES)
    return pl.pallas_call(
        functools.partial(pipeline, lax.axis_size("section")),
        out_shape=[jax.ShapeDtypeStruct((2, PAIR, HALF), jnp.bfloat16)] * 2,
        in_specs=[any_space] * 2,
        out_specs=[any_space] * 2,
        scratch_shapes=[
            pltpu.VMEM((2, PAIR, HALF), jnp.bfloat16),
            pltpu.VMEM((2, PAIR, HALF), jnp.bfloat16),
            pltpu.VMEM((PAIR, HALF), jnp.bfloat16),
            pltpu.VMEM((PAIR, HALF), jnp.float32),
            pltpu.VMEM((PAIR, HALF), jnp.bfloat16),
            pltpu.VMEM((PAIR, HALF), jnp.bfloat16),
            pltpu.VMEM((2, HALF, HALF), jnp.bfloat16),
            pltpu.VMEM((2, HALF, HALF), jnp.bfloat16),
            pltpu.VMEM((HALF, HALF), jnp.bfloat16),
            pltpu.VMEM((CHUNK, HALF), jnp.float32),
            dma((5,)),
            dma((2,)),
            dma((2,)),
        ]
        + [dma(pieces)] * 8,
        compiler_params=pltpu.CompilerParams(
            collective_id=0, has_side_effects=True, vmem_limit_bytes=56 * 2**20
        ),
        name="pipeline",
    )(source, matrix)


def compact(counts, rows):
    ends = jnp.cumsum(counts)
    at = jnp.arange(LIVE, dtype=jnp.int32)
    micro = jnp.sum((at[:, None] >= ends[None, :]).astype(jnp.int32), axis=1)
    begin = ends - counts
    slot = micro * ROWS + at - jnp.sum(
        jnp.where(micro[:, None] == jnp.arange(MICRO)[None, :], begin[None, :], 0), axis=1
    )
    chosen = (slot[:, None] == jnp.arange(TOK_DEV, dtype=jnp.int32)[None, :]).astype(jnp.bfloat16)
    return jnp.stack(
        [
            mm(chosen, rows[:, :HALF]).astype(jnp.bfloat16),
            mm(chosen, rows[:, HALF:]).astype(jnp.bfloat16),
        ]
    )


def shards(tokens, cotangent, live_counts, weight, inverse_in, inverse_out):
    section_here = lax.axis_index("section")
    rank_count = lax.axis_size("dp")
    core = lax.rem(lax.axis_index("dp"), 2)
    total = jnp.float32(TOK_DEV * rank_count)
    source = compact(live_counts[0], jnp.where(section_here == 0, tokens, cotangent))
    x_pair, s_pair = run_pipeline(source, weight[0])

    def own(pair):
        part = lax.dynamic_slice_in_dim(pair, core * LIVE, LIVE, 1)
        return jnp.concatenate([part[0], part[1]], axis=1)

    in_flat = own(x_pair)
    scaled_flat = own(s_pair)
    gram_in = block_gram(in_flat, total)
    gram_out = block_gram(scaled_flat, total)
    owned_in, owned_out = (
        lax.psum_scatter(
            gram_in.astype(jnp.bfloat16), "dp", scatter_dimension=0, tiled=True
        ).astype(jnp.float32),
        lax.psum_scatter(
            gram_out.astype(jnp.bfloat16), "dp", scatter_dimension=0, tiled=True
        ).astype(jnp.float32),
    )
    owned_rows = D // rank_count
    grad_rows = lax.psum_scatter(
        lax.dot_general(
            in_flat, scaled_flat, (((0,), (0,)), ((), ())), preferred_element_type=jnp.float32
        ).astype(jnp.bfloat16),
        "dp",
        scatter_dimension=0,
        tiled=True,
    ).astype(jnp.float32)
    left = jnp.einsum(
        "kbc,kcd->kbd",
        inverse_in[0],
        grad_rows.reshape(owned_rows // BLOCK, BLOCK, D),
        precision=lax.Precision.HIGHEST,
    )
    right = jnp.einsum(
        "rkc,kce->rke",
        left.reshape(owned_rows, NBLK, BLOCK),
        inverse_out[0],
        precision=lax.Precision.HIGHEST,
    )
    update = (right.reshape(owned_rows, D) / jnp.sqrt(total)).astype(jnp.bfloat16)
    return (update[None], owned_in[None], owned_out[None])


def solution(mesh):
    in_specs = (
        P("dp", None),
        P("dp", None),
        P("dp", None),
        P("section", None, None),
        P("section", "dp", None, None),
        P("section", None, None, None),
    )
    out_specs = (
        P("section", "dp", None),
        P("section", "dp", None, None),
        P("section", "dp", None, None),
    )
    return jax.shard_map(shards, mesh=mesh, in_specs=in_specs, out_specs=out_specs, check_vma=False)
```

time: 986 us -> 519 us (0.53)
  waiting for transfers between devices: 462 us -> 275 us
  Pallas kernels: 0 us -> 167 us
  other arithmetic: 175 us -> 9.37 us
  matrix products: 136 us -> 32.2 us
  starting transfers between devices: 97.7 us -> 0.3 us
  local copies, waits for them, and re-layouts: 92.4 us -> 17.5 us
    ppermute x22 -> x0, waiting for transfers between devices: 236 us -> none  [from_behind(): return lax.ppermute(x, axis, pairs)]
    pallas_call x0 -> x1, Pallas kernels: none -> 167 us  [run_pipeline(): pl.pallas_call(functools.partial(pipeline, lax.axis_size('section')), out...]
    dot_general x9 -> x3, matrix products: 113 us -> 14 us  [the longest x1 11.1 us: shards(): lax.dot_general(in_flat, scaled_flat, (((0,), (0,)), ((), ())), preferred...]
    ppermute x22 -> x0, starting transfers between devices: 97.2 us -> none  [from_behind(): return lax.ppermute(x, axis, pairs)]
    dynamic_update_slice x33 -> x0, other arithmetic: 73.8 us -> none  [the longest x11 36.1 us: backward_tick(): lax.dynamic_update_index_in_dim(stored_scaled, jnp.where(valid, scaled, o...]
    convert_element_type x24 -> x0, other arithmetic: 56.4 us -> none  [the longest x11 28.9 us: forward_tick(): result = (current.astype(jnp.float32) + activate(pre)).astype(jnp.bfloat16)]
    dynamic_slice x33 -> x0, local copies, waits for them, and re-layouts: 56.4 us -> none  [the longest x11 24.4 us: forward_tick(): old_pre = lax.dynamic_index_in_dim(stored_pre, index, 0, keepdims=False)]
    reduce_scatter x1, waiting for transfers between devices: 0.02 us -> 44.7 us  [shards(): lax.psum_scatter(gram_in.astype(jnp.bfloat16), 'dp', scatter_dimension=0,...]
  transfers between devices with their start and end apart: 25 -> 3, of which waited for: 24 -> 3; matrix products, arithmetic and copies ran while one was open for 24% -> 4% of each run, Pallas kernels for 0% -> 0%
where the time goes in v1:
time: 519 us; the launch traced here: 516 us
  waiting for transfers between devices  275 us (53%)
  Pallas kernels  167 us (32%)
  matrix products  32.2 us (6%)
  local copies, waits for them, and re-layouts  17.5 us (3%)
  between operations  13.8 us (3%)
  other arithmetic  9.37 us (2%)
    pallas_call x1, Pallas kernels, run_pipeline(): pl.pallas_call(functools.partial(pipeline, lax.axis_size('section')), out...  167 us
    reduce_scatter x1, waiting for transfers between devices, shards(): lax.psum_scatter(lax.dot_general(in_flat, scaled_flat, (((0,), (0,)), (()...  160 us
    reduce_scatter x1, waiting for transfers between devices, shards(): lax.psum_scatter(gram_out.astype(jnp.bfloat16), 'dp', scatter_dimension=0...  70.8 us
    reduce_scatter x1, waiting for transfers between devices, shards(): lax.psum_scatter(gram_in.astype(jnp.bfloat16), 'dp', scatter_dimension=0,...  44.7 us
    slice x5, local copies, waits for them, and re-layouts, own(): return jnp.concatenate([part[0], part[1]], axis=1)  12.5 us
    dot_general x1, matrix products, shards(): lax.dot_general(in_flat, scaled_flat, (((0,), (0,)), ((), ())), preferred...  11.1 us
  transfers between devices with their start and end apart: 3, of which 3 were waited for; matrix products, arithmetic and copies ran while one was open for 4% of the time, Pallas kernels for 0%

profile of v1, /device:TPU:5, one launch (start us, length us, event | category | flops | bytes accessed | tf_op | source)
XLA Modules:
  0.0 515.6 jit_solution(16535465910441510893)
XLA Ops:
  7.2 0.0 copy-start
  7.2 0.0 reduce-scatter.6.cloned.1.call-start
  7.2 1.0 reduce-window.4
  8.2 0.7 fusion.27
  8.9 0.1 convert_reduce_fusion
  9.0 0.1 select_reduce_fusion
  9.1 1.8 broadcast_select_fusion
  10.8 1.5 fusion.4
  12.3 1.5 fusion.3
  13.7 2.6 pad_maximum_fusion.source
  16.4 167.2 %pipeline.1 = (bf16[2,480,1536]{2,1,0:T(8,128)(2,1)}, bf16[2,480,1536]{2,1,0:T(8,128)(2,1)}) custom-call(bf16[2,240,1536]{2,1,0:T(8,128)(2,1)} %pad_maximum_fusion.source, bf16[3072,3072]{1,0:T(8,128)(2,1)} %bitcast.48), custom_call_target="tpu_custom_call" | custom-call | tf_op jit(solution)/shard_map/pipeline/pallas_call | solution.py:321
  183.6 3.4 constant_dynamic-slice_fusion
  187.1 2.3 copy.24
  189.3 2.3 copy.25
  191.6 4.1 multiply_convert_fusion.1
  195.7 0.0 reduce-scatter.6.cloned.1.call-update
  195.7 0.0 reduce-scatter.8.cloned.1.call-start
  195.7 2.3 copy.27
  198.0 2.3 copy.26
  200.3 4.1 multiply_convert_fusion
  204.4 0.0 reduce-scatter.8.cloned.1.call-update
  204.4 0.2 reduce-scatter.4.cloned.1.call-start
  204.6 11.1 %convolution_convert_fusion = bf16[3072,3072]{1,0:T(8,128)(2,1)} fusion(bf16[240,1536]{1,0:T(8,128)(2,1)} %bitcast.50, bf16[240,1536]{1,0:T(8,128)(2,1)} %bitcast.49, bf16[240,1536]{1,0:T(8,128)(2,1)} %bitcast.51, bf16[240,1536]{1,0:T(8,128)(2,1)} %bitcast.52), kind=kOutput, calls=%fused_computation | convolution fusion | flops 4545183744 | bytes 21823488 | tf_op jit(solution)/shard_map/dot_general | solution.py:392
  215.7 0.0 reduce-scatter.4.cloned.1.call-update
  215.7 0.0 copy-start.1
  215.7 44.7 %reduce-scatter.6.cloned.1.call-done = bf16[1,192,192]{2,1,0:T(8,128)(2,1)} async-done(((bf16[16,192,192]{2,1,0:T(8,128)(2,1)}), bf16[1,192,192]{2,1,0:T(8,128)(2,1)}) %reduce-scatter.6.cloned.1.call-update) | async-done | bytes 73744 | tf_op jit(solution)/shard_map/reduce_scatter | solution.py:383
  260.4 1.6 bitcast_convert_fusion.1
  262.0 70.8 %reduce-scatter.8.cloned.1.call-done = bf16[1,192,192]{2,1,0:T(8,128)(2,1)} async-done(((bf16[16,192,192]{2,1,0:T(8,128)(2,1)}), bf16[1,192,192]{2,1,0:T(8,128)(2,1)}) %reduce-scatter.8.cloned.1.call-update) | async-done | bytes 73744 | tf_op jit(solution)/shard_map/reduce_scatter | solution.py:386
  332.8 1.6 bitcast_convert_fusion
  334.3 159.6 %reduce-scatter.4.cloned.1.call-done = bf16[192,3072]{1,0:T(8,128)(2,1)} async-done(((bf16[3072,3072]{1,0:T(8,128)(2,1)}), bf16[192,3072]{1,0:T(8,128)(2,1)}) %reduce-scatter.4.cloned.1.call-update) | async-done | bytes 1179664 | tf_op jit(solution)/shard_map/reduce_scatter | solution.py:391
  494.0 2.5 copy.31
  496.5 0.0 copy-done.1
  496.5 2.8 fusion.23
  499.3 0.0 copy-done
  499.4 7.2 %multiply_convert_fusion.2 = bf16[16,192,192]{1,2,0:T(8,128)(2,1)} fusion(f32[1,16,192,192]{3,2,1,0:T(8,128)S(1)} %copy-done, f32[16,192,192]{2,1,0:T(8,128)S(1)} %fusion.23), kind=kOutput, calls=%fused_computation.6 | convolution fusion | flops 1360134144 | bytes 5898240 | tf_op jit(solution)/shard_map/rkc,kce->rke/dot_general | solution.py:405
  506.5 2.5 copy.28
  (1 shorter events, 0.0 us)
Async XLA Ops:
  7.2 492.2 %copy-start = (f32[1,16,192,192]{3,2,1,0:T(8,128)S(1)}, f32[1,16,192,192]{3,2,1,0:T(8,128)}, u32[]{:S(2)}) copy-start(f32[1,16,192,192]{3,2,1,0:T(8,128)} %param.11) | copy-start | bytes 7077892
  7.2 253.2 %reduce-scatter.6.cloned.1.call-start = ((), (), s32[]{:S(2)}) async-start(), calls=%async_computation.4 | async-start | bytes 1671168 | tf_op jit(solution)/shard_map/reduce_scatter | solution.py:383
  195.7 137.1 %reduce-scatter.8.cloned.1.call-start = ((), (), s32[]{:S(2)}) async-start(), calls=%async_computation.5 | async-start | bytes 1671168 | tf_op jit(solution)/shard_map/reduce_scatter | solution.py:386
  204.4 289.6 %reduce-scatter.4.cloned.1.call-start = ((), (), s32[]{:S(2)}) async-start(), calls=%async_computation.3 | async-start | bytes 20054016 | tf_op jit(solution)/shard_map/reduce_scatter | solution.py:391
  215.7 280.8 %copy-start.1 = (f32[1,1,192,192]{3,2,1,0:T(8,128)S(1)}, f32[1,1,192,192]{3,2,1,0:T(8,128)}, u32[]{:S(2)}) copy-start(f32[1,1,192,192]{3,2,1,0:T(8,128)} %param.10) | copy-start | bytes 442372
Sparse Core Ops, SparseCore 0:
  195.8 64.5 reduce-scatter.5
  264.8 67.8 reduce-scatter.7
  337.1 156.8 reduce-scatter.3

commit v2 on v1

v2 whole, which is shorter than its diff:
```python
import functools

import jax
import jax.numpy as jnp
from jax import lax
from jax.experimental import pallas as pl
from jax.experimental.pallas import tpu as pltpu
from jax.sharding import PartitionSpec as P

D = 3072
HALF = D // 2
BLOCK = 192
MICRO = 4
ROWS = 80
TOK_DEV = 320
LIVE = 240
NBLK = 16
PAIR = 2 * LIVE
CHUNK = 48
CHUNKS = PAIR // CHUNK
PIECES = 3
WIDTH = HALF // PIECES

C_ZERO = 0.7978845608028654
C_ONE = 0.044715
MESH = pl.DeviceIdType.MESH
RING = 4
QUAD = 4 * BLOCK
TWIN = 2 * BLOCK
TILES = HALF // TWIN
TOKENS = 5120


def activate(value):
    return 0.5 * value * (1.0 + jnp.tanh(C_ZERO * (value + C_ONE * value * value * value)))


def slope(value):
    hyper = jnp.tanh(C_ZERO * (value + C_ONE * value * value * value))
    return 0.5 * (1.0 + hyper) + 0.5 * value * (1.0 - hyper * hyper) * C_ZERO * (
        1.0 + 3.0 * C_ONE * value * value
    )


def mm(a, b):
    return jnp.dot(a, b, preferred_element_type=jnp.float32)


def gram(a, b):
    return lax.dot_general(a, b, (((0,), (0,)), ((), ())), preferred_element_type=jnp.float32)


def pipeline(
    stages,
    source,
    weight,
    inv_in,
    inv_out,
    update,
    gram_in,
    gram_out,
    x_buf,
    s_all,
    s_sib,
    g_buf,
    slopes,
    f_send,
    b_send,
    w_fwd,
    w_bwd,
    w_raw,
    acc,
    x_all,
    x_turned,
    d_send,
    d_recv,
    d_own,
    r_send,
    r_recv,
    p_raw,
    p_in,
    p_out,
    square,
    gi_send,
    gi_recv,
    go_send,
    go_recv,
    load_sem,
    init_send,
    init_recv,
    f_send_sem,
    f_recv_sem,
    b_send_sem,
    b_recv_sem,
    xs_send_sem,
    xs_recv_sem,
    ss_send_sem,
    ss_recv_sem,
    xa_send_sem,
    xa_recv_sem,
    sa_send_sem,
    sa_recv_sem,
    d_send_sem,
    d_recv_sem,
    r_send_sem,
    r_recv_sem,
    gi_sem,
    go_send_sem,
    go_recv_sem,
):
    stage = lax.axis_index("section")
    rank = lax.axis_index("dp")
    core = lax.rem(rank, 2)
    side = lax.rem(rank // 2, 2)
    ring = rank // 4
    sibling = {"dp": rank + 1 - 2 * core}
    across = {"dp": rank + 2 - 4 * side}
    last = stages - 1
    following = {"section": jnp.minimum(stage + 1, last)}
    previous = {"section": jnp.maximum(stage - 1, 0)}
    own_cols = pl.ds(pl.multiple_of(core * HALF, HALF), HALF)
    sib_cols = pl.ds(pl.multiple_of((1 - core) * HALF, HALF), HALF)

    def ring_at(d):
        return lax.rem(ring + d, RING)

    def ring_peer(d):
        return {"dp": ring_at(d) * 4 + lax.rem(rank, 4)}

    def go_rank(e):
        return (2 * core + ring // 2) * 4 + lax.rem(ring, 2) * 2 + e

    def go_source(h):
        return (2 * lax.rem(ring, 2) + side) * 4 + h * 2 + ring // 2

    loads = (
        pltpu.make_async_copy(weight.at[own_cols, own_cols], w_fwd.at[0], load_sem.at[0]),
        pltpu.make_async_copy(weight.at[sib_cols, own_cols], w_fwd.at[1], load_sem.at[1]),
        pltpu.make_async_copy(weight.at[own_cols, sib_cols], w_raw, load_sem.at[2]),
    )
    for load in loads:
        load.start()

    barrier = pltpu.get_barrier_semaphore()

    def greet(device):
        pl.semaphore_signal(barrier, inc=1, device_id=device, device_id_type=MESH)

    greet(sibling)
    greet(across)
    for d in range(1, RING):
        greet(ring_peer(d))

    @pl.when(stage > 0)
    def _():
        greet(previous)

    @pl.when(stage < last)
    def _():
        greet(following)

    for h in range(2):

        @pl.when(go_source(h) != rank)
        def _():
            greet({"dp": go_source(h)})

    expected = 5 + (stage > 0).astype(jnp.int32) + (stage < last).astype(jnp.int32)
    for e in range(2):
        expected = expected + (go_rank(e) != rank).astype(jnp.int32)
    pl.semaphore_wait(barrier, expected)

    mine = pl.ds(pl.multiple_of(core * LIVE, 16), LIVE)

    @pl.when(stage == 0)
    def _():
        moves = (
            pltpu.make_async_copy(source.at[core], x_buf.at[0, mine], load_sem.at[3]),
            pltpu.make_async_copy(source.at[1 - core], x_buf.at[1, mine], load_sem.at[4]),
            pltpu.make_async_remote_copy(
                source.at[1 - core], x_buf.at[0, mine], init_send.at[0], init_recv.at[0],
                device_id=sibling, device_id_type=MESH,
            ),
            pltpu.make_async_remote_copy(
                source.at[core], x_buf.at[1, mine], init_send.at[1], init_recv.at[1],
                device_id=sibling, device_id_type=MESH,
            ),
        )
        for move in moves:
            move.start()
        for move in moves:
            move.wait()

    @pl.when(stage == last)
    def _():
        moves = (
            pltpu.make_async_copy(source.at[core], g_buf.at[mine], load_sem.at[3]),
            pltpu.make_async_remote_copy(
                source.at[1 - core], g_buf.at[mine], init_send.at[0], init_recv.at[0],
                device_id=sibling, device_id_type=MESH,
            ),
        )
        for move in moves:
            move.start()
        for move in moves:
            move.wait()

    for load in loads:
        load.wait()

    def rows_of(k):
        return pl.ds(pl.multiple_of(k * CHUNK, 16), CHUNK)

    def cols_of(p):
        return pl.ds(p * WIDTH, WIDTH)

    def remote(src, dst, send, recv, device):
        return pltpu.make_async_remote_copy(
            src, dst, send, recv, device_id=device, device_id_type=MESH
        )

    def f_copy(k, p):
        at = (rows_of(k), cols_of(p))
        return remote(
            f_send.at[at], x_buf.at[(0,) + at], f_send_sem.at[k, p], f_recv_sem.at[k, p], following
        )

    def b_copy(k, p):
        at = (rows_of(k), cols_of(p))
        return remote(
            b_send.at[at], g_buf.at[at], b_send_sem.at[k, p], b_recv_sem.at[k, p], previous
        )

    def x_copy(k, p):
        at = (rows_of(k), cols_of(p))
        return remote(
            x_buf.at[(0,) + at], x_buf.at[(1,) + at], xs_send_sem.at[k, p], xs_recv_sem.at[k, p],
            sibling,
        )

    def s_copy(k, p):
        at = (rows_of(k), cols_of(p))
        return remote(
            s_all.at[(ring,) + at], s_sib.at[at], ss_send_sem.at[k, p], ss_recv_sem.at[k, p], sibling
        )

    def quad_of(r):
        which = jnp.where(r // 2 == core, 0, 1)
        return which, pl.ds(pl.multiple_of(lax.rem(r, 2) * QUAD, QUAD), QUAD)

    def xa_send(k, d):
        which, cols = quad_of(ring_at(d))
        return remote(
            x_buf.at[which, rows_of(k), cols], x_all.at[ring, rows_of(k)],
            xa_send_sem.at[k, d - 1], xa_recv_sem.at[k, d - 1], ring_peer(d),
        )

    def xa_recv(k, d):
        here = x_all.at[ring_at(RING - d), rows_of(k)]
        return remote(here, here, xa_send_sem.at[k, d - 1], xa_recv_sem.at[k, d - 1], ring_peer(d))

    def sa_send(k, d):
        here = s_all.at[ring, rows_of(k)]
        return remote(here, here, sa_send_sem.at[k, d - 1], sa_recv_sem.at[k, d - 1], ring_peer(d))

    def sa_recv(k, d):
        here = s_all.at[ring_at(RING - d), rows_of(k)]
        return remote(here, here, sa_send_sem.at[k, d - 1], sa_recv_sem.at[k, d - 1], ring_peer(d))

    def forward(k):
        rows = rows_of(k)
        for p in range(PIECES):
            cols = cols_of(p)

            @pl.when(stage > 0)
            def _():
                f_copy(k, p).wait_recv()
                x_copy(k, p).start()

            term = mm(x_buf[0, rows, cols], w_fwd[0, cols, :])
            acc[...] = term if p == 0 else acc[...] + term
        for p in range(PIECES):

            @pl.when(stage > 0)
            def _():
                x_copy(k, p).wait_recv()

            cols = cols_of(p)
            if p < PIECES - 1:
                acc[...] += mm(x_buf[1, rows, cols], w_fwd[1, cols, :])
        end = cols_of(PIECES - 1)
        for p in range(PIECES):
            cols = cols_of(p)
            pre = acc[:, cols] + mm(x_buf[1, rows, end], w_fwd[1, end, cols])
            slopes[rows, cols] = pre

            @pl.when(stage < last)
            def _():
                f_send[rows, cols] = (
                    x_buf[0, rows, cols].astype(jnp.float32) + activate(pre)
                ).astype(jnp.bfloat16)
                f_copy(k, p).start()

        for d in range(1, RING):
            xa_send(k, d).start()
        slopes[rows, :] = slope(slopes[rows, :])
        which, cols = quad_of(ring)
        x_all[ring, rows, :] = x_buf[which, rows, cols]

    def backward(k):
        rows = rows_of(k)
        for p in range(PIECES):
            cols = cols_of(p)

            @pl.when(stage < last)
            def _():
                b_copy(k, p).wait_recv()

            s_all[ring, rows, cols] = (
                g_buf[rows, cols].astype(jnp.float32) * slopes[rows, cols]
            ).astype(jnp.bfloat16)
            s_copy(k, p).start()

            @pl.when(stage > 0)
            def _():
                term = mm(s_all[ring, rows, cols], w_bwd[0, cols, :])
                acc[...] = term if p == 0 else acc[...] + term

        @pl.when(stage == 0)
        def _():
            for d in range(1, RING):
                sa_send(k, d).start()

        for p in range(PIECES):
            s_copy(k, p).wait_recv()
            cols = cols_of(p)
            if p < PIECES - 1:

                @pl.when(stage > 0)
                def _():
                    acc[...] += mm(s_sib[rows, cols], w_bwd[1, cols, :])

        @pl.when(stage > 0)
        def _():
            end = cols_of(PIECES - 1)
            for p in range(PIECES):
                cols = cols_of(p)
                back = acc[:, cols] + mm(s_sib[rows, end], w_bwd[1, end, cols])
                b_send[rows, cols] = (
                    g_buf[rows, cols].astype(jnp.float32) + back
                ).astype(jnp.bfloat16)
                b_copy(k, p).start()
            for d in range(1, RING):
                sa_send(k, d).start()

    turn_at = jnp.where(2 * stage + CHUNKS > 2 * last, 0, stage + CHUNKS)
    tile = 256

    def turn():
        @pl.when(stage > 0)
        def _():
            def step(i, carry):
                at = pl.ds(pl.multiple_of(i * tile, tile), tile)
                for j in range(HALF // tile):
                    to = pl.ds(j * tile, tile)
                    w_bwd[0, to, at] = w_fwd[0, at, to].T
                    w_bwd[1, to, at] = w_raw[at, to].T
                return carry

            lax.fori_loop(0, HALF // tile, step, 0)

        load = pltpu.make_async_copy(inv_in, p_raw.at[0], load_sem.at[0])
        load.start()
        load.wait()
        p_in[...] = p_raw[0].astype(jnp.bfloat16)
        p_out[...] = jnp.zeros_like(p_out)

        def step(i, carry):
            pair = pltpu.make_async_copy(inv_out.at[pl.ds(2 * i, 2)], p_raw, load_sem.at[0])
            pair.start()
            pair.wait()
            p_out[i, 0:BLOCK, 0:BLOCK] = p_raw[0].astype(jnp.bfloat16)
            p_out[i, BLOCK:TWIN, BLOCK:TWIN] = p_raw[1].astype(jnp.bfloat16)
            return carry

        lax.fori_loop(0, 2 * TILES, step, 0)

    def twin_of(h):
        return pl.ds(pl.multiple_of(h * TWIN, TWIN), TWIN)

    gi_copy = remote(gi_send, gi_recv, gi_sem.at[0], gi_sem.at[1], across)

    def collect_x():
        def arrive(k, carry):
            for d in range(1, RING):
                xa_recv(k, d).wait_recv()
            return carry

        lax.fori_loop(0, CHUNKS, arrive, 0)

        def turn_x(r, carry):
            for j in range(QUAD // tile):
                cols = pl.ds(j * tile, tile)
                x_turned[r, cols, :] = x_all[r, :, cols].T
            return carry

        lax.fori_loop(0, RING, turn_x, 0)
        for part in range(2):
            half = 1 - side if part == 0 else side
            rows = pl.ds(pl.multiple_of(half * TWIN + core * BLOCK, 16), BLOCK)
            both = jnp.zeros((BLOCK, TWIN), jnp.float32)
            for r in range(RING):
                both += mm(x_turned[r, rows, :], x_all[r, :, twin_of(half)])
            square[0:BLOCK, :] = both * (1.0 / TOKENS)
            target = gi_send if part == 0 else gram_in
            for e in range(2):

                @pl.when(core == e)
                def _():
                    target[...] = square[0:BLOCK, e * BLOCK : (e + 1) * BLOCK]

            if part == 0:
                gi_copy.start()

    collect_at = stage + CHUNKS + 6

    def slot(t, carry):
        @pl.when(t == turn_at)
        def _():
            turn()

        kf = t - stage

        @pl.when((kf >= 0) & (kf < CHUNKS))
        def _():
            forward(kf)

        kb = t - (2 * last - stage)

        @pl.when((kb >= 0) & (kb < CHUNKS))
        def _():
            backward(kb)

        @pl.when(t == collect_at)
        def _():
            collect_x()

        return carry

    lax.fori_loop(0, 2 * last + CHUNKS, slot, 0)

    def arrive(k, carry):
        for d in range(1, RING):
            sa_recv(k, d).wait_recv()
        return carry

    lax.fori_loop(0, CHUNKS, arrive, 0)

    def partial(half, j):
        cols = pl.ds(pl.multiple_of(j * TWIN, TWIN), TWIN)
        total = mm(x_turned[0, twin_of(half), :], s_all[0, :, cols])
        for r in range(1, RING):
            total += mm(x_turned[r, twin_of(half), :], s_all[r, :, cols])
        return total

    def d_copy(j):
        return remote(d_send.at[j], d_recv.at[j], d_send_sem.at[j], d_recv_sem.at[j], across)

    def r_copy(j):
        return remote(r_send.at[j], r_recv.at[j], r_send_sem.at[j], r_recv_sem.at[j], sibling)

    def theirs(j, carry):
        d_send[j] = partial(1 - side, j).astype(jnp.bfloat16)
        d_copy(j).start()
        return carry

    lax.fori_loop(0, TILES, theirs, 0)

    square[...] = jnp.zeros_like(square)
    for r in range(RING):
        cols = twin_of(ring)
        square[...] += gram(s_all[r, :, cols], s_all[r, :, cols])

    def go_remote(e, device):
        return remote(go_send.at[e], go_recv.at[side], go_send_sem.at[e], go_recv_sem.at[side], device)

    def go_local(e):
        return pltpu.make_async_copy(go_send.at[e], go_recv.at[side], go_recv_sem.at[side])

    for e in range(2):
        span = slice(e * BLOCK, (e + 1) * BLOCK)
        go_send[e] = square[span, span] * (1.0 / TOKENS)

        @pl.when(go_rank(e) == rank)
        def _():
            go_local(e).start()

        @pl.when(go_rank(e) != rank)
        def _():
            go_remote(e, {"dp": go_rank(e)}).start()

    def ours(j, carry):
        d_own[j] = partial(side, j)
        return carry

    lax.fori_loop(0, TILES, ours, 0)

    def condition(grad, which, j):
        left = mm(p_in[...], grad).astype(jnp.bfloat16)
        right = mm(left, p_out[which * TILES + j]) * (1.0 / TOKENS**0.5)
        at = pl.ds(pl.multiple_of(which * HALF + j * TWIN, TWIN), TWIN)
        update[:, at] = right.astype(jnp.bfloat16)

    def settle(j, carry):
        d_copy(j).wait_recv()
        d_own[j] = d_own[j] + d_recv[j].astype(jnp.float32)
        theirs_at = pl.ds(pl.multiple_of((1 - core) * BLOCK, 16), BLOCK)
        ours_at = pl.ds(pl.multiple_of(core * BLOCK, 16), BLOCK)
        r_send[j] = d_own[j, theirs_at, :].astype(jnp.bfloat16)
        r_copy(j).start()
        condition(d_own[j, ours_at, :].astype(jnp.bfloat16), core, j)
        return carry

    lax.fori_loop(0, TILES, settle, 0)

    def finish(j, carry):
        r_copy(j).wait_recv()
        condition(r_recv[j], 1 - core, j)
        return carry

    lax.fori_loop(0, TILES, finish, 0)

    gi_copy.wait()
    gram_in[...] += gi_recv[...]
    for h in range(2):
        own = go_source(h) == rank

        @pl.when(own)
        def _():
            pltpu.make_async_copy(go_send.at[0], go_recv.at[h], go_recv_sem.at[h]).wait()

        @pl.when(jnp.logical_not(own))
        def _():
            remote(
                go_send.at[0], go_recv.at[h], go_send_sem.at[0], go_recv_sem.at[h], sibling
            ).wait_recv()

    gram_out[...] = go_recv[0] + go_recv[1]

    def drain(k, carry):
        for p in range(PIECES):

            @pl.when(stage < last)
            def _():
                f_copy(k, p).wait_send()

            @pl.when(stage > 0)
            def _():
                x_copy(k, p).wait_send()
                b_copy(k, p).wait_send()

            s_copy(k, p).wait_send()
        for d in range(1, RING):
            xa_send(k, d).wait_send()
            sa_send(k, d).wait_send()
        return carry

    lax.fori_loop(0, CHUNKS, drain, 0)
    for j in range(TILES):
        d_copy(j).wait_send()
        r_copy(j).wait_send()
    for e in range(2):

        @pl.when(go_rank(e) != rank)
        def _():
            go_remote(e, sibling).wait_send()


def run_pipeline(source, matrix, inverse_in, inverse_out):
    dma = pltpu.SemaphoreType.DMA
    any_space = pl.BlockSpec(memory_space=pl.ANY)
    in_vmem = pl.BlockSpec(memory_space=pltpu.VMEM)
    pieces = (CHUNKS, PIECES)
    peers = (CHUNKS, RING - 1)
    bf16, f32 = jnp.bfloat16, jnp.float32
    return pl.pallas_call(
        functools.partial(pipeline, lax.axis_size("section")),
        out_shape=[
            jax.ShapeDtypeStruct((BLOCK, D), bf16),
            jax.ShapeDtypeStruct((BLOCK, BLOCK), f32),
            jax.ShapeDtypeStruct((BLOCK, BLOCK), f32),
        ],
        in_specs=[any_space] * 4,
        out_specs=[in_vmem] * 3,
        scratch_shapes=[
            pltpu.VMEM((2, PAIR, HALF), bf16),
            pltpu.VMEM((RING, PAIR, HALF), bf16),
            pltpu.VMEM((PAIR, HALF), bf16),
            pltpu.VMEM((PAIR, HALF), bf16),
            pltpu.VMEM((PAIR, HALF), f32),
            pltpu.VMEM((PAIR, HALF), bf16),
            pltpu.VMEM((PAIR, HALF), bf16),
            pltpu.VMEM((2, HALF, HALF), bf16),
            pltpu.VMEM((2, HALF, HALF), bf16),
            pltpu.VMEM((HALF, HALF), bf16),
            pltpu.VMEM((CHUNK, HALF), f32),
            pltpu.VMEM((RING, PAIR, QUAD), bf16),
            pltpu.VMEM((RING, QUAD, PAIR), bf16),
            pltpu.VMEM((TILES, TWIN, TWIN), bf16),
            pltpu.VMEM((TILES, TWIN, TWIN), bf16),
            pltpu.VMEM((TILES, TWIN, TWIN), f32),
            pltpu.VMEM((TILES, BLOCK, TWIN), bf16),
            pltpu.VMEM((TILES, BLOCK, TWIN), bf16),
            pltpu.VMEM((2, BLOCK, BLOCK), f32),
            pltpu.VMEM((BLOCK, BLOCK), bf16),
            pltpu.VMEM((2 * TILES, TWIN, TWIN), bf16),
            pltpu.VMEM((TWIN, TWIN), f32),
            pltpu.VMEM((BLOCK, BLOCK), f32),
            pltpu.VMEM((BLOCK, BLOCK), f32),
            pltpu.VMEM((2, BLOCK, BLOCK), f32),
            pltpu.VMEM((2, BLOCK, BLOCK), f32),
            dma((5,)),
            dma((2,)),
            dma((2,)),
        ]
        + [dma(pieces)] * 8
        + [dma(peers)] * 4
        + [dma((TILES,))] * 4
        + [dma((2,))] * 3,
        compiler_params=pltpu.CompilerParams(
            collective_id=0, has_side_effects=True, vmem_limit_bytes=62 * 2**20
        ),
        name="pipeline",
    )(source, matrix, inverse_in, inverse_out)


def compact(counts, rows):
    ends = jnp.cumsum(counts)
    at = jnp.arange(LIVE, dtype=jnp.int32)
    micro = jnp.sum((at[:, None] >= ends[None, :]).astype(jnp.int32), axis=1)
    begin = ends - counts
    slot = micro * ROWS + at - jnp.sum(
        jnp.where(micro[:, None] == jnp.arange(MICRO)[None, :], begin[None, :], 0), axis=1
    )
    chosen = (slot[:, None] == jnp.arange(TOK_DEV, dtype=jnp.int32)[None, :]).astype(jnp.bfloat16)
    return jnp.stack(
        [
            mm(chosen, rows[:, :HALF]).astype(jnp.bfloat16),
            mm(chosen, rows[:, HALF:]).astype(jnp.bfloat16),
        ]
    )


def shards(tokens, cotangent, live_counts, weight, inverse_in, inverse_out):
    section_here = lax.axis_index("section")
    source = compact(live_counts[0], jnp.where(section_here == 0, tokens, cotangent))
    update, owned_in, owned_out = run_pipeline(source, weight[0], inverse_in[0, 0], inverse_out[0])
    return (update[None], owned_in[None, None], owned_out[None, None])


def solution(mesh):
    in_specs = (
        P("dp", None),
        P("dp", None),
        P("dp", None),
        P("section", None, None),
        P("section", "dp", None, None),
        P("section", None, None, None),
    )
    out_specs = (
        P("section", "dp", None),
        P("section", "dp", None, None),
        P("section", "dp", None, None),
    )
    return jax.shard_map(shards, mesh=mesh, in_specs=in_specs, out_specs=out_specs, check_vma=False)
```

time: 519 us -> 226 us (0.44)
  waiting for transfers between devices: 275 us -> 0 us
  Pallas kernels: 167 us -> 211 us
  matrix products: 32.2 us -> 1.18 us
  local copies, waits for them, and re-layouts: 17.5 us -> 3.77 us
  between operations: 13.8 us -> 0.69 us
    reduce_scatter x3 -> x0, waiting for transfers between devices: 275 us -> none  [the longest x1 160 us: shards(): lax.psum_scatter(lax.dot_general(in_flat, scaled_flat, (((0,), (0,)), (()...]
    pallas_call x1, Pallas kernels: 167 us -> 211 us  [run_pipeline(): pl.pallas_call(functools.partial(pipeline, lax.axis_size('section')), out...]
    dot_general x5 -> x0, matrix products: 29.3 us -> none  [the longest x1 11.1 us: shards(): lax.dot_general(in_flat, scaled_flat, (((0,), (0,)), ((), ())), preferred...]
    slice x5 -> x0, local copies, waits for them, and re-layouts: 12.5 us -> none  [own(): return jnp.concatenate([part[0], part[1]], axis=1)]
  transfers between devices with their start and end apart: 3 -> 0, of which waited for: 3 -> 0; matrix products, arithmetic and copies ran while one was open for 4% -> 0% of each run, Pallas kernels for 0% -> 0%
where the time goes in v2:
time: 226 us; the launch traced here: 222 us
  Pallas kernels  211 us (93%)
  other arithmetic  4.69 us (2%)
  local copies, waits for them, and re-layouts  3.77 us (2%)
    pallas_call x1, Pallas kernels, run_pipeline(): pl.pallas_call(functools.partial(pipeline, lax.axis_size('section')), out...  211 us

profile of v2, /device:TPU:5, one launch (start us, length us, event | category | flops | bytes accessed | tf_op | source)
XLA Modules:
  0.0 221.6 jit_solution(2474889014371496145)
XLA Ops:
  0.6 0.8 reduce-window.4
  1.5 0.7 fusion.6
  2.1 0.1 convert_reduce_fusion
  2.2 0.1 select_reduce_fusion
  2.3 1.8 broadcast_select_fusion
  4.1 0.6 fusion.1
  4.7 0.6 fusion
  5.3 1.3 pad_maximum_fusion.source
  6.5 211.3 %pipeline.1 = (bf16[192,3072]{1,0:T(8,128)(2,1)}, f32[192,192]{1,0:T(8,128)}, f32[192,192]{1,0:T(8,128)}) custom-call(bf16[2,240,1536]{2,1,0:T(8,128)(2,1)} %pad_maximum_fusion.source, bf16[3072,3072]{1,0:T(8,128)(2,1)} %bitcast.18, f32[192,192]{1,0:T(8,128)} %bitcast.21, f32[16,192,192]{2,1,0:T(8,128)} %bitcast.19), custom_call_target="tpu_custom_call" | custom-call | tf_op jit(solution)/shard_map/pipeline/pallas_call | solution.py:586
  217.8 0.0 copy-start.1
  217.8 0.0 copy-start
  217.8 2.4 %copy.12 = bf16[1,192,3072]{2,1,0:T(8,128)(2,1)} copy(bf16[1,192,3072]{2,1,0:T(8,128)(2,1)} %bitcast.20) | data formatting | bytes 2359296
  220.2 0.0 copy-done.1
  220.2 0.7 copy.13
  220.9 0.0 copy-done
  220.9 0.7 copy.14
  (1 shorter events, 0.0 us)
Async XLA Ops:
  217.8 2.4 %copy-start.1 = (f32[192,192]{1,0:T(8,128)S(1)}, f32[192,192]{1,0:T(8,128)}, u32[]{:S(2)}) copy-start(f32[192,192]{1,0:T(8,128)} %get-tuple-element.7) | copy-start | bytes 442372
  217.8 3.1 %copy-start = (f32[192,192]{1,0:T(8,128)S(1)}, f32[192,192]{1,0:T(8,128)}, u32[]{:S(2)}) copy-start(f32[192,192]{1,0:T(8,128)} %get-tuple-element.8) | copy-start | bytes 442372

commit v3 on v2

v3 whole, which is shorter than its diff:
```python
import functools

import jax
import jax.numpy as jnp
from jax import lax
from jax.experimental import pallas as pl
from jax.experimental.pallas import tpu as pltpu
from jax.sharding import PartitionSpec as P

D = 3072
HALF = D // 2
BLOCK = 192
MICRO = 4
ROWS = 80
TOK_DEV = 320
LIVE = 240
NBLK = 16
PAIR = 2 * LIVE
CHUNK = 48
CHUNKS = PAIR // CHUNK
PIECES = 3
WIDTH = HALF // PIECES

C_ZERO = 0.7978845608028654
C_ONE = 0.044715
MESH = pl.DeviceIdType.MESH
RING = 4
QUAD = 4 * BLOCK
TWIN = 2 * BLOCK
CHIPS = 8
SHARE = CHUNKS // 2
SEEN = SHARE * CHIPS * CHUNK
TOKENS = 5120


def activate(value):
    return 0.5 * value * (1.0 + jnp.tanh(C_ZERO * (value + C_ONE * value * value * value)))


def slope(value):
    hyper = jnp.tanh(C_ZERO * (value + C_ONE * value * value * value))
    return 0.5 * (1.0 + hyper) + 0.5 * value * (1.0 - hyper * hyper) * C_ZERO * (
        1.0 + 3.0 * C_ONE * value * value
    )


def mm(a, b):
    return jnp.dot(a, b, preferred_element_type=jnp.float32)


def gram(a, b):
    return lax.dot_general(a, b, (((0,), (0,)), ((), ())), preferred_element_type=jnp.float32)


def pipeline(
    stages,
    source,
    weight,
    inv_in,
    inv_out,
    update,
    gram_in,
    gram_out,
    x_buf,
    s_buf,
    g_buf,
    slopes,
    h_send,
    w_fwd,
    w_bwd,
    w_raw,
    f_acc,
    b_acc,
    x_all,
    x_turned,
    s_all,
    e_send,
    e_recv,
    o_send,
    o_recv,
    p_raw,
    p_in,
    p_out,
    square,
    gi_send,
    gi_recv,
    go_send,
    go_recv,
    load_sem,
    init_send,
    init_recv,
    f_send_sem,
    f_recv_sem,
    b_send_sem,
    b_recv_sem,
    xs_send_sem,
    xs_recv_sem,
    ss_send_sem,
    ss_recv_sem,
    xa_send_sem,
    xa_recv_sem,
    sa_send_sem,
    sa_recv_sem,
    e_send_sem,
    e_recv_sem,
    o_send_sem,
    o_recv_sem,
    gi_sem,
    go_send_sem,
    go_recv_sem,
):
    stage = lax.axis_index("section")
    rank = lax.axis_index("dp")
    core = lax.rem(rank, 2)
    side = lax.rem(rank // 2, 2)
    ring = rank // 4
    upper = ring // 2
    quarter = 2 * lax.rem(ring, 2) + side
    chip = rank // 2
    sibling = {"dp": rank + 1 - 2 * core}
    last = stages - 1
    following = {"section": jnp.minimum(stage + 1, last)}
    previous = {"section": jnp.maximum(stage - 1, 0)}
    own_cols = pl.ds(pl.multiple_of(core * HALF, HALF), HALF)
    sib_cols = pl.ds(pl.multiple_of((1 - core) * HALF, HALF), HALF)

    def chip_at(d):
        return 2 * lax.rem(ring + d // 2, RING) + lax.rem(side + d, 2)

    def chip_before(d):
        return 2 * lax.rem(ring + RING - d // 2, RING) + lax.rem(side + d, 2)

    def go_rank(e):
        return quarter * 4 + upper * 2 + e

    def go_source(e):
        return (2 * side + ring // 2) * 4 + lax.rem(ring, 2) * 2 + e

    loads = (
        pltpu.make_async_copy(weight.at[own_cols, own_cols], w_fwd.at[0], load_sem.at[0]),
        pltpu.make_async_copy(weight.at[sib_cols, own_cols], w_fwd.at[1], load_sem.at[1]),
        pltpu.make_async_copy(weight.at[own_cols, sib_cols], w_raw, load_sem.at[2]),
    )
    for load in loads:
        load.start()

    barrier = pltpu.get_barrier_semaphore()

    def greet(device):
        pl.semaphore_signal(barrier, inc=1, device_id=device, device_id_type=MESH)

    greet(sibling)
    for d in range(1, CHIPS):
        greet({"dp": 2 * chip_at(d) + core})

    @pl.when(stage > 0)
    def _():
        greet(previous)

    @pl.when(stage < last)
    def _():
        greet(following)

    for e in range(2):

        @pl.when(go_source(e) != rank)
        def _():
            greet({"dp": go_source(e)})

    expected = CHIPS + (stage > 0).astype(jnp.int32) + (stage < last).astype(jnp.int32)
    for e in range(2):
        expected = expected + (go_rank(e) != rank).astype(jnp.int32)
    pl.semaphore_wait(barrier, expected)

    mine = pl.ds(pl.multiple_of(core * LIVE, 16), LIVE)

    def remote(src, dst, send, recv, device):
        return pltpu.make_async_remote_copy(
            src, dst, send, recv, device_id=device, device_id_type=MESH
        )

    @pl.when(stage == 0)
    def _():
        moves = (
            pltpu.make_async_copy(source.at[core], x_buf.at[0, mine], load_sem.at[3]),
            pltpu.make_async_copy(source.at[1 - core], x_buf.at[1, mine], load_sem.at[4]),
            remote(
                source.at[1 - core], x_buf.at[0, mine], init_send.at[0], init_recv.at[0], sibling
            ),
            remote(source.at[core], x_buf.at[1, mine], init_send.at[1], init_recv.at[1], sibling),
        )
        for move in moves:
            move.start()
        for move in moves:
            move.wait()

    @pl.when(stage == last)
    def _():
        moves = (
            pltpu.make_async_copy(source.at[core], g_buf.at[mine], load_sem.at[3]),
            remote(source.at[1 - core], g_buf.at[mine], init_send.at[0], init_recv.at[0], sibling),
        )
        for move in moves:
            move.start()
        for move in moves:
            move.wait()

    for load in loads:
        load.wait()

    def rows_of(k):
        return pl.ds(pl.multiple_of(k * CHUNK, 16), CHUNK)

    def cols_of(p):
        return pl.ds(p * WIDTH, WIDTH)

    def f_copy(k, p):
        at = (rows_of(k), cols_of(p))
        return remote(
            h_send.at[at], x_buf.at[(0,) + at], f_send_sem.at[k, p], f_recv_sem.at[k, p], following
        )

    def b_copy(k, p):
        at = (rows_of(k), cols_of(p))
        return remote(
            h_send.at[at], g_buf.at[at], b_send_sem.at[k, p], b_recv_sem.at[k, p], previous
        )

    def x_copy(k, p):
        at = (rows_of(k), cols_of(p))
        return remote(
            x_buf.at[(0,) + at], x_buf.at[(1,) + at], xs_send_sem.at[k, p], xs_recv_sem.at[k, p],
            sibling,
        )

    def s_copy(k, p):
        at = (rows_of(k), cols_of(p))
        return remote(
            s_buf.at[(0,) + at], s_buf.at[(1,) + at], ss_send_sem.at[k, p], ss_recv_sem.at[k, p],
            sibling,
        )

    def x_part(to, k):
        which = jnp.where(to // 4 == core, 0, 1)
        return x_buf.at[which, rows_of(k)]

    def s_part(to, k):
        which = jnp.where(lax.rem(to // 2, 2) == core, 0, 1)
        cols = pl.ds(pl.multiple_of(lax.rem(to, 2) * QUAD, QUAD), QUAD)
        return s_buf.at[which, rows_of(k), cols]

    def slot_of(i, who):
        return pl.ds(pl.multiple_of((i * CHIPS + who) * CHUNK, 16), CHUNK)

    def xa_send(k, d):
        i = k // 2
        return remote(
            x_part(chip_at(d), k), x_all.at[slot_of(i, chip)],
            xa_send_sem.at[i, d - 1], xa_recv_sem.at[i, d - 1], {"dp": 2 * chip_at(d) + core},
        )

    def xa_recv(i, d):
        here = x_all.at[slot_of(i, chip_before(d))]
        return remote(here, here, xa_send_sem.at[i, d - 1], xa_recv_sem.at[i, d - 1], sibling)

    def sa_send(k, d):
        i = k // 2
        return remote(
            s_part(chip_at(d), k), s_all.at[slot_of(i, chip)],
            sa_send_sem.at[i, d - 1], sa_recv_sem.at[i, d - 1], {"dp": 2 * chip_at(d) + core},
        )

    def sa_recv(i, d):
        here = s_all.at[slot_of(i, chip_before(d))]
        return remote(here, here, sa_send_sem.at[i, d - 1], sa_recv_sem.at[i, d - 1], sibling)

    end = cols_of(PIECES - 1)

    def forward_own(k):
        rows = rows_of(k)
        for p in range(PIECES):
            cols = cols_of(p)

            @pl.when(stage > 0)
            def _():
                f_copy(k, p).wait_recv()
                x_copy(k, p).start()

            term = mm(x_buf[0, rows, cols], w_fwd[0, cols, :])
            f_acc[...] = term if p == 0 else f_acc[...] + term

    def forward_rest(k):
        rows = rows_of(k)
        for p in range(PIECES):

            @pl.when(stage > 0)
            def _():
                x_copy(k, p).wait_recv()

            cols = cols_of(p)
            if p < PIECES - 1:
                f_acc[...] += mm(x_buf[1, rows, cols], w_fwd[1, cols, :])
        for p in range(PIECES):
            cols = cols_of(p)
            pre = f_acc[:, cols] + mm(x_buf[1, rows, end], w_fwd[1, end, cols])
            slopes[rows, cols] = pre

            @pl.when(stage < last)
            def _():
                h_send[rows, cols] = (
                    x_buf[0, rows, cols].astype(jnp.float32) + activate(pre)
                ).astype(jnp.bfloat16)
                f_copy(k, p).start()

    def forward_end(k):
        rows = rows_of(k)
        slopes[rows, :] = slope(slopes[rows, :])

        @pl.when(lax.rem(k, 2) == core)
        def _():
            for d in range(1, CHIPS):
                xa_send(k, d).start()
            which = jnp.where(upper == core, 0, 1)
            x_all[slot_of(k // 2, chip), :] = x_buf[which, rows, :]

    def backward_start(k):
        rows = rows_of(k)
        for p in range(PIECES):
            cols = cols_of(p)

            @pl.when(stage < last)
            def _():
                b_copy(k, p).wait_recv()

            s_buf[0, rows, cols] = (
                g_buf[rows, cols].astype(jnp.float32) * slopes[rows, cols]
            ).astype(jnp.bfloat16)
            s_copy(k, p).start()

    def backward_own(k):
        @pl.when(stage > 0)
        def _():
            rows = rows_of(k)
            b_acc[...] = mm(s_buf[0, rows, :], w_bwd[0])

    def backward_rest(k):
        rows = rows_of(k)
        for p in range(PIECES):
            s_copy(k, p).wait_recv()
            cols = cols_of(p)
            if p < PIECES - 1:

                @pl.when(stage > 0)
                def _():
                    b_acc[...] += mm(s_buf[1, rows, cols], w_bwd[1, cols, :])

        @pl.when(stage > 0)
        def _():
            @pl.when(stage < last)
            def _():
                for p in range(PIECES):
                    f_copy(k, p).wait_send()

            for p in range(PIECES):
                cols = cols_of(p)
                back = b_acc[:, cols] + mm(s_buf[1, rows, end], w_bwd[1, end, cols])
                h_send[rows, cols] = (
                    g_buf[rows, cols].astype(jnp.float32) + back
                ).astype(jnp.bfloat16)
                b_copy(k, p).start()

    def backward_end(k):
        @pl.when(lax.rem(k, 2) == core)
        def _():
            for d in range(1, CHIPS):
                sa_send(k, d).start()
            which = jnp.where(lax.rem(ring, 2) == core, 0, 1)
            cols = pl.ds(pl.multiple_of(side * QUAD, QUAD), QUAD)
            s_all[slot_of(k // 2, chip), :] = s_buf[which, rows_of(k), cols]

    turn_at = jnp.where(2 * stage + CHUNKS > 2 * last, 0, stage + CHUNKS)
    tile = 256

    def turn():
        @pl.when(stage > 0)
        def _():
            def step(i, carry):
                at = pl.ds(pl.multiple_of(i * tile, tile), tile)
                for j in range(HALF // tile):
                    to = pl.ds(j * tile, tile)
                    w_bwd[0, to, at] = w_fwd[0, at, to].T
                    w_bwd[1, to, at] = w_raw[at, to].T
                return carry

            lax.fori_loop(0, HALF // tile, step, 0)

        load = pltpu.make_async_copy(inv_in, p_raw.at[0], load_sem.at[0])
        load.start()
        load.wait()
        p_in[...] = p_raw[0].astype(jnp.bfloat16)
        p_out[...] = jnp.zeros_like(p_out)

        def step(i, carry):
            pair = pltpu.make_async_copy(inv_out.at[pl.ds(2 * i, 2)], p_raw, load_sem.at[0])
            pair.start()
            pair.wait()
            p_out[i, 0:BLOCK, 0:BLOCK] = p_raw[0].astype(jnp.bfloat16)
            p_out[i, BLOCK:TWIN, BLOCK:TWIN] = p_raw[1].astype(jnp.bfloat16)
            return carry

        lax.fori_loop(0, NBLK // 2, step, 0)

    gi_copy = remote(gi_send, gi_recv, gi_sem.at[0], gi_sem.at[1], sibling)

    def collect_x():
        def arrive(i, carry):
            for d in range(1, CHIPS):
                xa_recv(i, d).wait_recv()
            return carry

        lax.fori_loop(0, SHARE, arrive, 0)

        def turn_x(j, carry):
            cols = pl.ds(pl.multiple_of(j * tile, tile), tile)
            x_turned[cols, :] = x_all[:, cols].T
            return carry

        lax.fori_loop(0, HALF // tile, turn_x, 0)
        at = pl.ds(pl.multiple_of(quarter * TWIN, TWIN), TWIN)
        square[...] = mm(x_turned[at, :], x_all[:, at]) * (1.0 / TOKENS)
        for e in range(2):
            span = slice(e * BLOCK, (e + 1) * BLOCK)

            @pl.when(core == e)
            def _():
                gram_in[...] = square[span, span]

            @pl.when(core != e)
            def _():
                gi_send[...] = square[span, span]

        gi_copy.start()

    slots = 2 * last + CHUNKS + 1
    collect_at = jnp.where(stage == 0, CHUNKS, slots - stage)

    def slot(t, carry):
        @pl.when(t == turn_at)
        def _():
            turn()

        @pl.when(t == collect_at)
        def _():
            collect_x()

        kf = t - stage
        kb = t - (2 * last + 1 - stage)
        has_f = (kf >= 0) & (kf < CHUNKS)
        has_b = (kb >= 0) & (kb < CHUNKS)

        pl.when(has_b)(lambda: backward_start(kb))
        pl.when(has_f)(lambda: forward_own(kf))
        pl.when(has_b)(lambda: backward_own(kb))
        pl.when(has_f)(lambda: forward_rest(kf))
        pl.when(has_b)(lambda: backward_rest(kb))
        pl.when(has_f)(lambda: forward_end(kf))
        pl.when(has_b)(lambda: backward_end(kb))
        return carry

    lax.fori_loop(0, slots, slot, 0)

    def arrive(i, carry):
        for d in range(1, CHIPS):
            sa_recv(i, d).wait_recv()
        return carry

    lax.fori_loop(0, SHARE, arrive, 0)

    def block(j, parity):
        rows = pl.ds(pl.multiple_of((2 * j + parity) * BLOCK, 16), BLOCK)
        return mm(x_turned[rows, :], s_all[...])

    def e_copy(n):
        return remote(e_send.at[n], e_recv.at[n], e_send_sem.at[n], e_recv_sem.at[n], sibling)

    def o_copy(n, j):
        owner = {"dp": (2 * upper + j // 2) * 4 + lax.rem(j, 2) * 2 + core}
        return remote(
            o_send.at[n], o_recv.at[quarter], o_send_sem.at[n], o_recv_sem.at[quarter], owner
        )

    def reduce(n, carry):
        j = lax.rem(quarter + 1 + n, 4)
        e_send[n] = block(j, 1 - core).astype(jnp.bfloat16)
        e_copy(n).start()
        ours = block(j, core)
        e_copy(n).wait_recv()
        whole = (ours + e_recv[n].astype(jnp.float32)).astype(jnp.bfloat16)

        @pl.when(n < 3)
        def _():
            o_send[n] = whole
            o_copy(n, j).start()

        @pl.when(n == 3)
        def _():
            o_recv[quarter] = whole

        return carry

    lax.fori_loop(0, 4, reduce, 0)

    cols = pl.ds(pl.multiple_of(upper * TWIN, TWIN), TWIN)
    square[...] = gram(s_all[:, cols], s_all[:, cols]) * (1.0 / TOKENS)

    def go_remote(e, device):
        return remote(go_send.at[e], go_recv.at[core], go_send_sem.at[e], go_recv_sem.at[core], device)

    for e in range(2):
        span = slice(e * BLOCK, (e + 1) * BLOCK)
        go_send[e] = square[span, span]

        @pl.when(go_rank(e) == rank)
        def _():
            pltpu.make_async_copy(go_send.at[e], go_recv.at[core], go_recv_sem.at[core]).start()

        @pl.when(go_rank(e) != rank)
        def _():
            go_remote(e, {"dp": go_rank(e)}).start()

    def condition(n, carry):
        who = lax.rem(quarter + 4 - n, 4)

        @pl.when(n > 0)
        def _():
            here = o_recv.at[who]
            remote(here, here, o_send_sem.at[0], o_recv_sem.at[who], sibling).wait_recv()

        left = mm(p_in[...], o_recv[who]).astype(jnp.bfloat16)
        for j in range(2):
            right = mm(left[:, j * TWIN : (j + 1) * TWIN], p_out[2 * who + j])
            at = pl.ds(pl.multiple_of(who * QUAD + j * TWIN, TWIN), TWIN)
            update[:, at] = (right * (1.0 / TOKENS**0.5)).astype(jnp.bfloat16)
        return carry

    lax.fori_loop(0, 4, condition, 0)

    gi_copy.wait()
    gram_in[...] += gi_recv[...]
    for e in range(2):
        own = go_source(e) == rank

        @pl.when(own)
        def _():
            pltpu.make_async_copy(go_send.at[0], go_recv.at[e], go_recv_sem.at[e]).wait()

        @pl.when(jnp.logical_not(own))
        def _():
            here = go_recv.at[e]
            remote(here, here, go_send_sem.at[0], go_recv_sem.at[e], sibling).wait_recv()

    gram_out[...] = go_recv[0] + go_recv[1]

    def drain(k, carry):
        for p in range(PIECES):

            @pl.when((stage < last) & (stage == 0))
            def _():
                f_copy(k, p).wait_send()

            @pl.when(stage > 0)
            def _():
                x_copy(k, p).wait_send()
                b_copy(k, p).wait_send()

            s_copy(k, p).wait_send()

        @pl.when(lax.rem(k, 2) == core)
        def _():
            for d in range(1, CHIPS):
                xa_send(k, d).wait_send()
                sa_send(k, d).wait_send()

        return carry

    lax.fori_loop(0, CHUNKS, drain, 0)
    for n in range(4):
        e_copy(n).wait_send()
    for n in range(3):
        o_copy(n, lax.rem(quarter + 1 + n, 4)).wait_send()
    for e in range(2):

        @pl.when(go_rank(e) != rank)
        def _():
            go_remote(e, sibling).wait_send()


def run_pipeline(source, matrix, inverse_in, inverse_out):
    dma = pltpu.SemaphoreType.DMA
    any_space = pl.BlockSpec(memory_space=pl.ANY)
    in_vmem = pl.BlockSpec(memory_space=pltpu.VMEM)
    pieces = (CHUNKS, PIECES)
    peers = (SHARE, CHIPS - 1)
    bf16, f32 = jnp.bfloat16, jnp.float32
    return pl.pallas_call(
        functools.partial(pipeline, lax.axis_size("section")),
        out_shape=[
            jax.ShapeDtypeStruct((BLOCK, D), bf16),
            jax.ShapeDtypeStruct((BLOCK, BLOCK), f32),
            jax.ShapeDtypeStruct((BLOCK, BLOCK), f32),
        ],
        in_specs=[any_space] * 4,
        out_specs=[in_vmem] * 3,
        scratch_shapes=[
            pltpu.VMEM((2, PAIR, HALF), bf16),
            pltpu.VMEM((2, PAIR, HALF), bf16),
            pltpu.VMEM((PAIR, HALF), bf16),
            pltpu.VMEM((PAIR, HALF), f32),
            pltpu.VMEM((PAIR, HALF), bf16),
            pltpu.VMEM((2, HALF, HALF), bf16),
            pltpu.VMEM((2, HALF, HALF), bf16),
            pltpu.VMEM((HALF, HALF), bf16),
            pltpu.VMEM((CHUNK, HALF), f32),
            pltpu.VMEM((CHUNK, HALF), f32),
            pltpu.VMEM((SEEN, HALF), bf16),
            pltpu.VMEM((HALF, SEEN), bf16),
            pltpu.VMEM((SEEN, QUAD), bf16),
            pltpu.VMEM((4, BLOCK, QUAD), bf16),
            pltpu.VMEM((4, BLOCK, QUAD), bf16),
            pltpu.VMEM((3, BLOCK, QUAD), bf16),
            pltpu.VMEM((4, BLOCK, QUAD), bf16),
            pltpu.VMEM((2, BLOCK, BLOCK), f32),
            pltpu.VMEM((BLOCK, BLOCK), bf16),
            pltpu.VMEM((NBLK // 2, TWIN, TWIN), bf16),
            pltpu.VMEM((TWIN, TWIN), f32),
            pltpu.VMEM((BLOCK, BLOCK), f32),
            pltpu.VMEM((BLOCK, BLOCK), f32),
            pltpu.VMEM((2, BLOCK, BLOCK), f32),
            pltpu.VMEM((2, BLOCK, BLOCK), f32),
            dma((5,)),
            dma((2,)),
            dma((2,)),
        ]
        + [dma(pieces)] * 8
        + [dma(peers)] * 4
        + [dma((4,))] * 4
        + [dma((2,))] * 3,
        compiler_params=pltpu.CompilerParams(
            collective_id=0, has_side_effects=True, vmem_limit_bytes=62 * 2**20
        ),
        name="pipeline",
    )(source, matrix, inverse_in, inverse_out)


def compact(counts, rows):
    ends = jnp.cumsum(counts)
    at = jnp.arange(LIVE, dtype=jnp.int32)
    micro = jnp.sum((at[:, None] >= ends[None, :]).astype(jnp.int32), axis=1)
    begin = ends - counts
    slot = micro * ROWS + at - jnp.sum(
        jnp.where(micro[:, None] == jnp.arange(MICRO)[None, :], begin[None, :], 0), axis=1
    )
    chosen = (slot[:, None] == jnp.arange(TOK_DEV, dtype=jnp.int32)[None, :]).astype(jnp.bfloat16)
    return jnp.stack(
        [
            mm(chosen, rows[:, :HALF]).astype(jnp.bfloat16),
            mm(chosen, rows[:, HALF:]).astype(jnp.bfloat16),
        ]
    )


def shards(tokens, cotangent, live_counts, weight, inverse_in, inverse_out):
    section_here = lax.axis_index("section")
    source = compact(live_counts[0], jnp.where(section_here == 0, tokens, cotangent))
    update, owned_in, owned_out = run_pipeline(source, weight[0], inverse_in[0, 0], inverse_out[0])
    return (update[None], owned_in[None, None], owned_out[None, None])


def solution(mesh):
    in_specs = (
        P("dp", None),
        P("dp", None),
        P("dp", None),
        P("section", None, None),
        P("section", "dp", None, None),
        P("section", None, None, None),
    )
    out_specs = (
        P("section", "dp", None),
        P("section", "dp", None, None),
        P("section", "dp", None, None),
    )
    return jax.shard_map(shards, mesh=mesh, in_specs=in_specs, out_specs=out_specs, check_vma=False)
```

time: 226 us -> 268 us (1.19)
  Pallas kernels: 211 us -> 254 us
    pallas_call x1, Pallas kernels: 211 us -> 254 us  [run_pipeline(): pl.pallas_call(functools.partial(pipeline, lax.axis_size('section')), out...]
where the time goes in v3:
time: 268 us; the launch traced here: 265 us
  Pallas kernels  254 us (95%)
  other arithmetic  4.69 us (2%)
  local copies, waits for them, and re-layouts  3.77 us (1%)
    pallas_call x1, Pallas kernels, run_pipeline(): pl.pallas_call(functools.partial(pipeline, lax.axis_size('section')), out...  254 us

profile of v3, /device:TPU:5, one launch (start us, length us, event | category | flops | bytes accessed | tf_op | source)
XLA Modules:
  0.0 264.8 jit_solution(11880331600828137241)
XLA Ops:
  0.6 0.8 reduce-window.4
  1.5 0.7 fusion.6
  2.1 0.1 convert_reduce_fusion
  2.2 0.1 select_reduce_fusion
  2.3 1.8 broadcast_select_fusion
  4.1 0.6 fusion.1
  4.7 0.6 fusion
  5.3 1.3 pad_maximum_fusion.source
  6.5 254.5 %pipeline.1 = (bf16[192,3072]{1,0:T(8,128)(2,1)}, f32[192,192]{1,0:T(8,128)}, f32[192,192]{1,0:T(8,128)}) custom-call(bf16[2,240,1536]{2,1,0:T(8,128)(2,1)} %pad_maximum_fusion.source, bf16[3072,3072]{1,0:T(8,128)(2,1)} %bitcast.18, f32[192,192]{1,0:T(8,128)} %bitcast.21, f32[16,192,192]{2,1,0:T(8,128)} %bitcast.19), custom_call_target="tpu_custom_call" | custom-call | tf_op jit(solution)/shard_map/pipeline/pallas_call | solution.py:605
  261.0 0.0 copy-start.1
  261.0 0.0 copy-start
  261.0 2.4 copy.12
  263.4 0.0 copy-done.1
  263.4 0.7 copy.13
  264.1 0.0 copy-done
  264.1 0.7 copy.14
  (1 shorter events, 0.0 us)
Async XLA Ops:
  261.0 2.4 copy-start.1
  261.0 3.1 %copy-start = (f32[192,192]{1,0:T(8,128)S(1)}, f32[192,192]{1,0:T(8,128)}, u32[]{:S(2)}) copy-start(f32[192,192]{1,0:T(8,128)} %get-tuple-element.8) | copy-start | bytes 442372

commit v4 on v3

--- a/solution.py
+++ b/solution.py
@@ -29,6 +29,7 @@
 TWIN = 2 * BLOCK
 CHIPS = 8
 SHARE = CHUNKS // 2
+AHEAD = 6
 SEEN = SHARE * CHIPS * CHUNK
 TOKENS = 5120
 
@@ -54,7 +55,9 @@
 
 def pipeline(
     stages,
-    source,
+    counts,
+    tokens,
+    cotangent,
     weight,
     inv_in,
     inv_out,
@@ -69,8 +72,7 @@
     w_fwd,
     w_bwd,
     w_raw,
-    f_acc,
-    b_acc,
+    acc,
     x_all,
     x_turned,
     s_all,
@@ -136,6 +138,17 @@
     def go_source(e):
         return (2 * side + ring // 2) * 4 + lax.rem(ring, 2) * 2 + e
 
+    def staged(which):
+        return x_turned.at[pl.ds(pl.multiple_of(which * TOK_DEV, 16), TOK_DEV), pl.ds(0, HALF)]
+
+    def fetch(array):
+        return [
+            pltpu.make_async_copy(
+                array.at[:, pl.ds(h * HALF, HALF)], staged(h), load_sem.at[3 + h]
+            )
+            for h in range(2)
+        ]
+
     loads = (
         pltpu.make_async_copy(weight.at[own_cols, own_cols], w_fwd.at[0], load_sem.at[0]),
         pltpu.make_async_copy(weight.at[sib_cols, own_cols], w_fwd.at[1], load_sem.at[1]),
@@ -144,6 +157,16 @@
     for load in loads:
         load.start()
 
+    @pl.when(stage == 0)
+    def _():
+        for move in fetch(tokens):
+            move.start()
+
+    @pl.when(stage == last)
+    def _():
+        for move in fetch(cotangent):
+            move.start()
+
     barrier = pltpu.get_barrier_semaphore()
 
     def greet(device):
@@ -172,44 +195,64 @@
         expected = expected + (go_rank(e) != rank).astype(jnp.int32)
     pl.semaphore_wait(barrier, expected)
 
-    mine = pl.ds(pl.multiple_of(core * LIVE, 16), LIVE)
-
     def remote(src, dst, send, recv, device):
         return pltpu.make_async_remote_copy(
             src, dst, send, recv, device_id=device, device_id_type=MESH
         )
 
+    def rows_of(k):
+        return pl.ds(pl.multiple_of(k * CHUNK, 16), CHUNK)
+
+    def i_copy(k, h):
+        return remote(
+            x_buf.at[h, rows_of(k)], x_buf.at[1 - h, rows_of(k)],
+            xs_send_sem.at[k, h], xs_recv_sem.at[k, h], sibling,
+        )
+
+    mine = pl.ds(pl.multiple_of(core * LIVE, 16), LIVE)
+
+    def chosen():
+        slots = lax.broadcasted_iota(jnp.int32, (LIVE, TOK_DEV), 1)
+        places = jnp.full((LIVE, TOK_DEV), -1, jnp.int32)
+        begin = jnp.int32(0)
+        for m in range(MICRO):
+            count = counts[m]
+            slot = slots - m * ROWS
+            places = jnp.where((slot >= 0) & (slot < count), begin + slot, places)
+            begin = begin + count
+        return (places == lax.broadcasted_iota(jnp.int32, (LIVE, TOK_DEV), 0)).astype(jnp.bfloat16)
+
+    def picked(pick, which):
+        return mm(pick, staged(which)[...]).astype(jnp.bfloat16)
+
     @pl.when(stage == 0)
     def _():
-        moves = (
-            pltpu.make_async_copy(source.at[core], x_buf.at[0, mine], load_sem.at[3]),
-            pltpu.make_async_copy(source.at[1 - core], x_buf.at[1, mine], load_sem.at[4]),
-            remote(
-                source.at[1 - core], x_buf.at[0, mine], init_send.at[0], init_recv.at[0], sibling
-            ),
-            remote(source.at[core], x_buf.at[1, mine], init_send.at[1], init_recv.at[1], sibling),
-        )
-        for move in moves:
-            move.start()
-        for move in moves:
+        for move in fetch(tokens):
             move.wait()
+        pick = chosen()
+        x_buf[0, mine, :] = picked(pick, core)
+        x_buf[1, mine, :] = picked(pick, 1 - core)
+
+        def give(n, carry):
+            for h in range(2):
+                i_copy(core * SHARE + n, h).start()
+            return carry
+
+        lax.fori_loop(0, SHARE, give, 0)
 
     @pl.when(stage == last)
     def _():
-        moves = (
-            pltpu.make_async_copy(source.at[core], g_buf.at[mine], load_sem.at[3]),
-            remote(source.at[1 - core], g_buf.at[mine], init_send.at[0], init_recv.at[0], sibling),
-        )
-        for move in moves:
-            move.start()
-        for move in moves:
+        for move in fetch(cotangent):
             move.wait()
+        pick = chosen()
+        g_buf[mine, :] = picked(pick, core)
+        h_send[mine, :] = picked(pick, 1 - core)
+        give = remote(h_send.at[mine], g_buf.at[mine], init_send.at[0], init_recv.at[0], sibling)
+        give.start()
+        give.wait()
 
     for load in loads:
         load.wait()
-
-    def rows_of(k):
-        return pl.ds(pl.multiple_of(k * CHUNK, 16), CHUNK)
 
     def cols_of(p):
         return pl.ds(p * WIDTH, WIDTH)
@@ -240,6 +283,17 @@
             sibling,
         )
 
+    hold_x = (stage == last // 2) | (stage == last)
+    hold_s = stage == last // 2 + 1
+
+    def held(send):
+        def step(i, carry):
+            for d in range(1, CHIPS, 2):
+                send(2 * i + core, d).start()
+            return carry
+
+        lax.fori_loop(0, SHARE, step, 0)
+
     def x_part(to, k):
         which = jnp.where(to // 4 == core, 0, 1)
         return x_buf.at[which, rows_of(k)]
@@ -278,6 +332,12 @@
 
     def forward_own(k):
         rows = rows_of(k)
+
+        @pl.when((stage == 0) & (k // SHARE != core))
+        def _():
+            for h in range(2):
+                i_copy(k, h).wait_recv()
+
         for p in range(PIECES):
             cols = cols_of(p)
 
@@ -287,7 +347,7 @@
                 x_copy(k, p).start()
 
             term = mm(x_buf[0, rows, cols], w_fwd[0, cols, :])
-            f_acc[...] = term if p == 0 else f_acc[...] + term
+            acc[...] = term if p == 0 else acc[...] + term
 
     def forward_rest(k):
         rows = rows_of(k)
@@ -299,10 +359,10 @@
 
             cols = cols_of(p)
             if p < PIECES - 1:
-                f_acc[...] += mm(x_buf[1, rows, cols], w_fwd[1, cols, :])
+                acc[...] += mm(x_buf[1, rows, cols], w_fwd[1, cols, :])
         for p in range(PIECES):
             cols = cols_of(p)
-            pre = f_acc[:, cols] + mm(x_buf[1, rows, end], w_fwd[1, end, cols])
+            pre = acc[:, cols] + mm(x_buf[1, rows, end], w_fwd[1, end, cols])
             slopes[rows, cols] = pre
 
             @pl.when(stage < last)
@@ -318,8 +378,14 @@
 
         @pl.when(lax.rem(k, 2) == core)
         def _():
-            for d in range(1, CHIPS):
+            for d in range(2, CHIPS, 2):
                 xa_send(k, d).start()
+
+            @pl.when(jnp.logical_not(hold_x))
+            def _():
+                for d in range(1, CHIPS, 2):
+                    xa_send(k, d).start()
+
             which = jnp.where(upper == core, 0, 1)
             x_all[slot_of(k // 2, chip), :] = x_buf[which, rows, :]
 
@@ -341,7 +407,7 @@
         @pl.when(stage > 0)
         def _():
             rows = rows_of(k)
-            b_acc[...] = mm(s_buf[0, rows, :], w_bwd[0])
+            acc[...] = mm(s_buf[0, rows, :], w_bwd[0])
 
     def backward_rest(k):
         rows = rows_of(k)
@@ -352,7 +418,7 @@
 
                 @pl.when(stage > 0)
                 def _():
-                    b_acc[...] += mm(s_buf[1, rows, cols], w_bwd[1, cols, :])
+                    acc[...] += mm(s_buf[1, rows, cols], w_bwd[1, cols, :])
 
         @pl.when(stage > 0)
         def _():
@@ -363,7 +429,7 @@
 
             for p in range(PIECES):
                 cols = cols_of(p)
-                back = b_acc[:, cols] + mm(s_buf[1, rows, end], w_bwd[1, end, cols])
+                back = acc[:, cols] + mm(s_buf[1, rows, end], w_bwd[1, end, cols])
                 h_send[rows, cols] = (
                     g_buf[rows, cols].astype(jnp.float32) + back
                 ).astype(jnp.bfloat16)
@@ -372,13 +438,18 @@
     def backward_end(k):
         @pl.when(lax.rem(k, 2) == core)
         def _():
-            for d in range(1, CHIPS):
+            for d in range(2, CHIPS, 2):
                 sa_send(k, d).start()
+
+            @pl.when(jnp.logical_not(hold_s))
+            def _():
+                for d in range(1, CHIPS, 2):
+                    sa_send(k, d).start()
+
             which = jnp.where(lax.rem(ring, 2) == core, 0, 1)
             cols = pl.ds(pl.multiple_of(side * QUAD, QUAD), QUAD)
             s_all[slot_of(k // 2, chip), :] = s_buf[which, rows_of(k), cols]
 
-    turn_at = jnp.where(2 * stage + CHUNKS > 2 * last, 0, stage + CHUNKS)
     tile = 256
 
     def turn():
@@ -441,33 +512,50 @@
 
         gi_copy.start()
 
-    slots = 2 * last + CHUNKS + 1
-    collect_at = jnp.where(stage == 0, CHUNKS, slots - stage)
+    ahead = jnp.where(stage == last, 1, jnp.where(stage == last - 1, AHEAD, CHUNKS))
 
     def slot(t, carry):
-        @pl.when(t == turn_at)
+        @pl.when(t < CHUNKS)
+        def _():
+            forward_own(t)
+            forward_rest(t)
+            forward_end(t)
+
+        @pl.when((t == CHUNKS - 1) & hold_x)
+        def _():
+            held(xa_send)
+
+        @pl.when((t == CHUNKS - 1) & (2 * stage + CHUNKS <= 2 * last))
         def _():
             turn()
 
-        @pl.when(t == collect_at)
+        @pl.when((t == CHUNKS - 1) & (stage == 0))
         def _():
             collect_x()
 
-        kf = t - stage
-        kb = t - (2 * last + 1 - stage)
-        has_f = (kf >= 0) & (kf < CHUNKS)
-        has_b = (kb >= 0) & (kb < CHUNKS)
-
-        pl.when(has_b)(lambda: backward_start(kb))
-        pl.when(has_f)(lambda: forward_own(kf))
-        pl.when(has_b)(lambda: backward_own(kb))
-        pl.when(has_f)(lambda: forward_rest(kf))
-        pl.when(has_b)(lambda: backward_rest(kb))
-        pl.when(has_f)(lambda: forward_end(kf))
-        pl.when(has_b)(lambda: backward_end(kb))
+        @pl.when(t >= ahead - 1)
+        def _():
+            kb = t - (ahead - 1)
+            backward_start(kb)
+            backward_own(kb)
+            backward_rest(kb)
+            backward_end(kb)
+
         return carry
 
-    lax.fori_loop(0, slots, slot, 0)
+    @pl.when(2 * stage + CHUNKS > 2 * last)
+    def _():
+        turn()
+
+    lax.fori_loop(0, CHUNKS + ahead - 1, slot, 0)
+
+    @pl.when(hold_s)
+    def _():
+        held(sa_send)
+
+    @pl.when(stage > 0)
+    def _():
+        collect_x()
 
     def arrive(i, carry):
         for d in range(1, CHIPS):
@@ -575,6 +663,11 @@
 
             s_copy(k, p).wait_send()
 
+        @pl.when((stage == 0) & (k // SHARE == core))
+        def _():
+            for h in range(2):
+                i_copy(k, h).wait_send()
+
         @pl.when(lax.rem(k, 2) == core)
         def _():
             for d in range(1, CHIPS):
@@ -595,7 +688,7 @@
             go_remote(e, sibling).wait_send()
 
 
-def run_pipeline(source, matrix, inverse_in, inverse_out):
+def run_pipeline(counts, tokens, cotangent, matrix, inverse_in, inverse_out):
     dma = pltpu.SemaphoreType.DMA
     any_space = pl.BlockSpec(memory_space=pl.ANY)
     in_vmem = pl.BlockSpec(memory_space=pltpu.VMEM)
@@ -609,7 +702,7 @@
             jax.ShapeDtypeStruct((BLOCK, BLOCK), f32),
             jax.ShapeDtypeStruct((BLOCK, BLOCK), f32),
         ],
-        in_specs=[any_space] * 4,
+        in_specs=[pl.BlockSpec(memory_space=pltpu.SMEM)] + [any_space] * 5,
         out_specs=[in_vmem] * 3,
         scratch_shapes=[
             pltpu.VMEM((2, PAIR, HALF), bf16),
@@ -620,7 +713,6 @@
             pltpu.VMEM((2, HALF, HALF), bf16),
             pltpu.VMEM((2, HALF, HALF), bf16),
             pltpu.VMEM((HALF, HALF), bf16),
-            pltpu.VMEM((CHUNK, HALF), f32),
             pltpu.VMEM((CHUNK, HALF), f32),
             pltpu.VMEM((SEEN, HALF), bf16),
             pltpu.VMEM((HALF, SEEN), bf16),
@@ -638,8 +730,8 @@
             pltpu.VMEM((2, BLOCK, BLOCK), f32),
             pltpu.VMEM((2, BLOCK, BLOCK), f32),
             dma((5,)),
-            dma((2,)),
-            dma((2,)),
+            dma((1,)),
+            dma((1,)),
         ]
         + [dma(pieces)] * 8
         + [dma(peers)] * 4
@@ -649,30 +741,13 @@
             collective_id=0, has_side_effects=True, vmem_limit_bytes=62 * 2**20
         ),
         name="pipeline",
-    )(source, matrix, inverse_in, inverse_out)
-
-
-def compact(counts, rows):
-    ends = jnp.cumsum(counts)
-    at = jnp.arange(LIVE, dtype=jnp.int32)
-    micro = jnp.sum((at[:, None] >= ends[None, :]).astype(jnp.int32), axis=1)
-    begin = ends - counts
-    slot = micro * ROWS + at - jnp.sum(
-        jnp.where(micro[:, None] == jnp.arange(MICRO)[None, :], begin[None, :], 0), axis=1
+    )(counts, tokens, cotangent, matrix, inverse_in, inverse_out)
+
+
+def shards(tokens, cotangent, live_counts, weight, inverse_in, inverse_out):
+    update, owned_in, owned_out = run_pipeline(
+        live_counts[0], tokens, cotangent, weight[0], inverse_in[0, 0], inverse_out[0]
     )
-    chosen = (slot[:, None] == jnp.arange(TOK_DEV, dtype=jnp.int32)[None, :]).astype(jnp.bfloat16)
-    return jnp.stack(
-        [
-            mm(chosen, rows[:, :HALF]).astype(jnp.bfloat16),
-            mm(chosen, rows[:, HALF:]).astype(jnp.bfloat16),
-        ]
-    )
-
-
-def shards(tokens, cotangent, live_counts, weight, inverse_in, inverse_out):
-    section_here = lax.axis_index("section")
-    source = compact(live_counts[0], jnp.where(section_here == 0, tokens, cotangent))
-    update, owned_in, owned_out = run_pipeline(source, weight[0], inverse_in[0, 0], inverse_out[0])
     return (update[None], owned_in[None, None], owned_out[None, None])
 
 

time: 268 us -> 211 us (0.79)
  the two profiles are of different devices: /device:TPU:5 before, /device:TPU:103 now
where the time goes in v4:
time: 211 us
  Pallas kernels  206 us (98%)
  local copies, waits for them, and re-layouts  3.77 us (2%)
    pallas_call x1, Pallas kernels, run_pipeline(): pl.pallas_call(functools.partial(pipeline, lax.axis_size('section')), out...  206 us

profile of v4, /device:TPU:103, one launch (start us, length us, event | category | flops | bytes accessed | tf_op | source)
XLA Modules:
  0.0 210.9 jit_solution(14822146186823869576)
XLA Ops:
  0.6 206.4 %pipeline.1 = (bf16[192,3072]{1,0:T(8,128)(2,1)}, f32[192,192]{1,0:T(8,128)}, f32[192,192]{1,0:T(8,128)}) custom-call(s32[4]{0:T(128)} %bitcast.13, bf16[320,3072]{1,0:T(8,128)(2,1)} %tokens.1, bf16[320,3072]{1,0:T(8,128)(2,1)} %cotangent.1, bf16[3072,3072]{1,0:T(8,128)(2,1)} %bitcast.7, f32[192,192]{1,0:T(8,128)} %bitcast.10, f32[16,192,192]{2,1,0:T(8,128)} %bitcast.8), custom_call_target="tpu_custom_call" | custom-call | tf_op jit(solution)/shard_map/pipeline/pallas_call | solution.py:698
  207.1 0.0 copy-start.1
  207.1 0.0 copy-start
  207.1 2.4 %copy.12 = bf16[1,192,3072]{2,1,0:T(8,128)(2,1)} copy(bf16[1,192,3072]{2,1,0:T(8,128)(2,1)} %bitcast.9) | data formatting | bytes 2359296
  209.5 0.0 copy-done.1
  209.5 0.7 copy.13
  210.2 0.0 copy-done
  210.2 0.7 copy.14
Async XLA Ops:
  207.1 2.4 %copy-start.1 = (f32[192,192]{1,0:T(8,128)S(1)}, f32[192,192]{1,0:T(8,128)}, u32[]{:S(2)}) copy-start(f32[192,192]{1,0:T(8,128)} %get-tuple-element.7) | copy-start | bytes 442372
  207.1 3.1 %copy-start = (f32[192,192]{1,0:T(8,128)S(1)}, f32[192,192]{1,0:T(8,128)}, u32[]{:S(2)}) copy-start(f32[192,192]{1,0:T(8,128)} %get-tuple-element.8) | copy-start | bytes 442372

commit v5 on v4

--- a/solution.py
+++ b/solution.py
@@ -18,7 +18,7 @@
 PAIR = 2 * LIVE
 CHUNK = 48
 CHUNKS = PAIR // CHUNK
-PIECES = 3
+PIECES = 2
 WIDTH = HALF // PIECES
 
 C_ZERO = 0.7978845608028654
@@ -30,6 +30,9 @@
 CHIPS = 8
 SHARE = CHUNKS // 2
 AHEAD = 6
+HELD = 3
+DIRECT = (1, 5)
+INDIRECT = (3, 7)
 SEEN = SHARE * CHIPS * CHUNK
 TOKENS = 5120
 
@@ -101,6 +104,7 @@
     ss_recv_sem,
     xa_send_sem,
     xa_recv_sem,
+    xp_send_sem,
     sa_send_sem,
     sa_recv_sem,
     e_send_sem,
@@ -283,16 +287,9 @@
             sibling,
         )
 
-    hold_x = (stage == last // 2) | (stage == last)
+    hold_x = stage == last // 2
     hold_s = stage == last // 2 + 1
-
-    def held(send):
-        def step(i, carry):
-            for d in range(1, CHIPS, 2):
-                send(2 * i + core, d).start()
-            return carry
-
-        lax.fori_loop(0, SHARE, step, 0)
+    passing = hold_x | hold_s
 
     def x_part(to, k):
         which = jnp.where(to // 4 == core, 0, 1)
@@ -316,6 +313,24 @@
     def xa_recv(i, d):
         here = x_all.at[slot_of(i, chip_before(d))]
         return remote(here, here, xa_send_sem.at[i, d - 1], xa_recv_sem.at[i, d - 1], sibling)
+
+    def pass_on(i, d):
+        here = x_all.at[slot_of(i, chip_before(d))]
+        beside = ring + 1 - 2 * lax.rem(ring, 2)
+        away = lax.rem(beside - ring + d // 2 + RING, RING)
+        return remote(
+            here, here, xp_send_sem.at[i, d // 4], xa_recv_sem.at[i, 2 * away],
+            {"dp": 4 * beside + lax.rem(rank, 4)},
+        )
+
+    def pass_all():
+        def step(i, carry):
+            for d in DIRECT:
+                xa_recv(i, d).wait_recv()
+                pass_on(i, d).start()
+            return carry
+
+        lax.fori_loop(0, SHARE, step, 0)
 
     def sa_send(k, d):
         i = k // 2
@@ -383,7 +398,12 @@
 
             @pl.when(jnp.logical_not(hold_x))
             def _():
-                for d in range(1, CHIPS, 2):
+                for d in DIRECT:
+                    xa_send(k, d).start()
+
+            @pl.when(jnp.logical_not(passing))
+            def _():
+                for d in INDIRECT:
                     xa_send(k, d).start()
 
             which = jnp.where(upper == core, 0, 1)
@@ -441,7 +461,7 @@
             for d in range(2, CHIPS, 2):
                 sa_send(k, d).start()
 
-            @pl.when(jnp.logical_not(hold_s))
+            @pl.when(jnp.logical_not(hold_s) | (k < HELD))
             def _():
                 for d in range(1, CHIPS, 2):
                     sa_send(k, d).start()
@@ -485,8 +505,14 @@
 
     def collect_x():
         def arrive(i, carry):
-            for d in range(1, CHIPS):
+            for d in (2, 4, 6) + INDIRECT:
                 xa_recv(i, d).wait_recv()
+
+            @pl.when(jnp.logical_not(passing))
+            def _():
+                for d in DIRECT:
+                    xa_recv(i, d).wait_recv()
+
             return carry
 
         lax.fori_loop(0, SHARE, arrive, 0)
@@ -523,7 +549,16 @@
 
         @pl.when((t == CHUNKS - 1) & hold_x)
         def _():
-            held(xa_send)
+            def step(i, carry):
+                for d in DIRECT:
+                    xa_send(2 * i + core, d).start()
+                return carry
+
+            lax.fori_loop(0, SHARE, step, 0)
+
+        @pl.when((t == CHUNKS - 1) & passing)
+        def _():
+            pass_all()
 
         @pl.when((t == CHUNKS - 1) & (2 * stage + CHUNKS <= 2 * last))
         def _():
@@ -551,7 +586,15 @@
 
     @pl.when(hold_s)
     def _():
-        held(sa_send)
+        def step(k, carry):
+            @pl.when(lax.rem(k, 2) == core)
+            def _():
+                for d in range(1, CHIPS, 2):
+                    sa_send(k, d).start()
+
+            return carry
+
+        lax.fori_loop(HELD, CHUNKS, step, 0)
 
     @pl.when(stage > 0)
     def _():
@@ -577,10 +620,15 @@
             o_send.at[n], o_recv.at[quarter], o_send_sem.at[n], o_recv_sem.at[quarter], owner
         )
 
+    def share(n, carry):
+        e_send[n] = block(lax.rem(quarter + 1 + n, 4), 1 - core).astype(jnp.bfloat16)
+        e_copy(n).start()
+        return carry
+
+    lax.fori_loop(0, 4, share, 0)
+
     def reduce(n, carry):
         j = lax.rem(quarter + 1 + n, 4)
-        e_send[n] = block(j, 1 - core).astype(jnp.bfloat16)
-        e_copy(n).start()
         ours = block(j, core)
         e_copy(n).wait_recv()
         whole = (ours + e_recv[n].astype(jnp.float32)).astype(jnp.bfloat16)
@@ -631,8 +679,48 @@
             update[:, at] = (right * (1.0 / TOKENS**0.5)).astype(jnp.bfloat16)
         return carry
 
-    lax.fori_loop(0, 4, condition, 0)
-
+    lax.fori_loop(0, 1, condition, 0)
+
+    def drain(k, carry):
+        for p in range(PIECES):
+
+            @pl.when((stage < last) & (stage == 0))
+            def _():
+                f_copy(k, p).wait_send()
+
+            @pl.when(stage > 0)
+            def _():
+                x_copy(k, p).wait_send()
+                b_copy(k, p).wait_send()
+
+            s_copy(k, p).wait_send()
+
+        @pl.when((stage == 0) & (k // SHARE == core))
+        def _():
+            for h in range(2):
+                i_copy(k, h).wait_send()
+
+        @pl.when(lax.rem(k, 2) == core)
+        def _():
+            for d in range(1, CHIPS):
+                sa_send(k, d).wait_send()
+            for d in (2, 4, 6) + DIRECT:
+                xa_send(k, d).wait_send()
+
+            @pl.when(passing)
+            def _():
+                for d in DIRECT:
+                    pass_on(k // 2, d).wait_send()
+
+            @pl.when(jnp.logical_not(passing))
+            def _():
+                for d in INDIRECT:
+                    xa_send(k, d).wait_send()
+
+
+        return carry
+
+    lax.fori_loop(0, CHUNKS, drain, 0)
     gi_copy.wait()
     gram_in[...] += gi_recv[...]
     for e in range(2):
@@ -649,34 +737,8 @@
 
     gram_out[...] = go_recv[0] + go_recv[1]
 
-    def drain(k, carry):
-        for p in range(PIECES):
-
-            @pl.when((stage < last) & (stage == 0))
-            def _():
-                f_copy(k, p).wait_send()
-
-            @pl.when(stage > 0)
-            def _():
-                x_copy(k, p).wait_send()
-                b_copy(k, p).wait_send()
-
-            s_copy(k, p).wait_send()
-
-        @pl.when((stage == 0) & (k // SHARE == core))
-        def _():
-            for h in range(2):
-                i_copy(k, h).wait_send()
-
-        @pl.when(lax.rem(k, 2) == core)
-        def _():
-            for d in range(1, CHIPS):
-                xa_send(k, d).wait_send()
-                sa_send(k, d).wait_send()
-
-        return carry
-
-    lax.fori_loop(0, CHUNKS, drain, 0)
+    lax.fori_loop(1, 4, condition, 0)
+
     for n in range(4):
         e_copy(n).wait_send()
     for n in range(3):
@@ -734,7 +796,9 @@
             dma((1,)),
         ]
         + [dma(pieces)] * 8
-        + [dma(peers)] * 4
+        + [dma(peers)] * 2
+        + [dma((SHARE, 2))]
+        + [dma(peers)] * 2
         + [dma((4,))] * 4
         + [dma((2,))] * 3,
         compiler_params=pltpu.CompilerParams(

time: 211 us -> 200 us (0.948)
  the two profiles are of different devices: /device:TPU:103 before, /device:TPU:5 now
where the time goes in v5:
time: 200 us; the launch traced here: 199 us
  Pallas kernels  195 us (98%)
  local copies, waits for them, and re-layouts  3.77 us (2%)
    pallas_call x1, Pallas kernels, run_pipeline(): pl.pallas_call(functools.partial(pipeline, lax.axis_size('section')), out...  195 us

profile of v5, /device:TPU:5, one launch (start us, length us, event | category | flops | bytes accessed | tf_op | source)
XLA Modules:
  0.0 199.1 jit_solution(4358201514620904143)
XLA Ops:
  0.6 194.6 %pipeline.1 = (bf16[192,3072]{1,0:T(8,128)(2,1)}, f32[192,192]{1,0:T(8,128)}, f32[192,192]{1,0:T(8,128)}) custom-call(s32[4]{0:T(128)} %bitcast.13, bf16[320,3072]{1,0:T(8,128)(2,1)} %tokens.1, bf16[320,3072]{1,0:T(8,128)(2,1)} %cotangent.1, bf16[3072,3072]{1,0:T(8,128)(2,1)} %bitcast.7, f32[192,192]{1,0:T(8,128)} %bitcast.10, f32[16,192,192]{2,1,0:T(8,128)} %bitcast.8), custom_call_target="tpu_custom_call" | custom-call | tf_op jit(solution)/shard_map/pipeline/pallas_call | solution.py:760
  195.3 0.0 copy-start.1
  195.3 0.0 copy-start
  195.3 2.4 %copy.12 = bf16[1,192,3072]{2,1,0:T(8,128)(2,1)} copy(bf16[1,192,3072]{2,1,0:T(8,128)(2,1)} %bitcast.9) | data formatting | bytes 2359296
  197.7 0.0 copy-done.1
  197.7 0.7 copy.13
  198.4 0.0 copy-done
  198.4 0.7 copy.14
Async XLA Ops:
  195.3 2.4 %copy-start.1 = (f32[192,192]{1,0:T(8,128)S(1)}, f32[192,192]{1,0:T(8,128)}, u32[]{:S(2)}) copy-start(f32[192,192]{1,0:T(8,128)} %get-tuple-element.7) | copy-start | bytes 442372
  195.3 3.1 %copy-start = (f32[192,192]{1,0:T(8,128)S(1)}, f32[192,192]{1,0:T(8,128)}, u32[]{:S(2)}) copy-start(f32[192,192]{1,0:T(8,128)} %get-tuple-element.8) | copy-start | bytes 442372

commit v6 on v5

--- a/solution.py
+++ b/solution.py
@@ -81,7 +81,6 @@
     s_all,
     e_send,
     e_recv,
-    o_send,
     o_recv,
     p_raw,
     p_in,
@@ -158,7 +157,7 @@
         pltpu.make_async_copy(weight.at[sib_cols, own_cols], w_fwd.at[1], load_sem.at[1]),
         pltpu.make_async_copy(weight.at[own_cols, sib_cols], w_raw, load_sem.at[2]),
     )
-    for load in loads:
+    for load in loads[:2]:
         load.start()
 
     @pl.when(stage == 0)
@@ -255,8 +254,9 @@
         give.start()
         give.wait()
 
-    for load in loads:
+    for load in loads[:2]:
         load.wait()
+    loads[2].start()
 
     def cols_of(p):
         return pl.ds(p * WIDTH, WIDTH)
@@ -345,8 +345,11 @@
 
     end = cols_of(PIECES - 1)
 
-    def forward_own(k):
-        rows = rows_of(k)
+    def wide_rows(k, span):
+        return pl.ds(pl.multiple_of(k * CHUNK, 16), span * CHUNK)
+
+    def forward_own(k, span):
+        rows, some = wide_rows(k, span), pl.ds(0, span * CHUNK)
 
         @pl.when((stage == 0) & (k // SHARE != core))
         def _():
@@ -358,121 +361,148 @@
 
             @pl.when(stage > 0)
             def _():
-                f_copy(k, p).wait_recv()
-                x_copy(k, p).start()
+                for q in range(span):
+                    f_copy(k + q, p).wait_recv()
+                    x_copy(k + q, p).start()
 
             term = mm(x_buf[0, rows, cols], w_fwd[0, cols, :])
-            acc[...] = term if p == 0 else acc[...] + term
-
-    def forward_rest(k):
-        rows = rows_of(k)
+            acc[some, :] = term if p == 0 else acc[some, :] + term
+
+    def forward_rest(k, span):
+        rows, some = wide_rows(k, span), pl.ds(0, span * CHUNK)
         for p in range(PIECES):
 
             @pl.when(stage > 0)
             def _():
-                x_copy(k, p).wait_recv()
+                for q in range(span):
+                    x_copy(k + q, p).wait_recv()
 
             cols = cols_of(p)
             if p < PIECES - 1:
-                acc[...] += mm(x_buf[1, rows, cols], w_fwd[1, cols, :])
+                acc[some, :] += mm(x_buf[1, rows, cols], w_fwd[1, cols, :])
         for p in range(PIECES):
             cols = cols_of(p)
-            pre = acc[:, cols] + mm(x_buf[1, rows, end], w_fwd[1, end, cols])
-            slopes[rows, cols] = pre
-
-            @pl.when(stage < last)
-            def _():
-                h_send[rows, cols] = (
-                    x_buf[0, rows, cols].astype(jnp.float32) + activate(pre)
-                ).astype(jnp.bfloat16)
-                f_copy(k, p).start()
-
-    def forward_end(k):
-        rows = rows_of(k)
-        slopes[rows, :] = slope(slopes[rows, :])
-
-        @pl.when(lax.rem(k, 2) == core)
-        def _():
-            for d in range(2, CHIPS, 2):
-                xa_send(k, d).start()
-
-            @pl.when(jnp.logical_not(hold_x))
-            def _():
-                for d in DIRECT:
-                    xa_send(k, d).start()
-
-            @pl.when(jnp.logical_not(passing))
-            def _():
-                for d in INDIRECT:
-                    xa_send(k, d).start()
-
-            which = jnp.where(upper == core, 0, 1)
-            x_all[slot_of(k // 2, chip), :] = x_buf[which, rows, :]
-
-    def backward_start(k):
-        rows = rows_of(k)
+            pre = acc[some, cols] + mm(x_buf[1, rows, end], w_fwd[1, end, cols])
+            acc[some, cols] = pre
+            if span == 1:
+
+                @pl.when(stage < last)
+                def _():
+                    h_send[rows, cols] = (
+                        x_buf[0, rows, cols].astype(jnp.float32) + activate(pre)
+                    ).astype(jnp.bfloat16)
+                    f_copy(k, p).start()
+
+    def forward_end(k, span):
+        rows = wide_rows(k, span)
+        slopes[rows, :] = slope(acc[pl.ds(0, span * CHUNK), :]).astype(jnp.bfloat16)
+        for q in range(span):
+
+            @pl.when(lax.rem(k + q, 2) == core)
+            def _():
+                for d in range(2, CHIPS, 2):
+                    xa_send(k + q, d).start()
+
+                @pl.when(jnp.logical_not(hold_x))
+                def _():
+                    for d in DIRECT:
+                        xa_send(k + q, d).start()
+
+                @pl.when(jnp.logical_not(passing))
+                def _():
+                    for d in INDIRECT:
+                        xa_send(k + q, d).start()
+
+                which = jnp.where(upper == core, 0, 1)
+                x_all[slot_of((k + q) // 2, chip), :] = x_buf[which, rows_of(k + q), :]
+
+    def backward_start(k, span):
+        rows = wide_rows(k, span)
         for p in range(PIECES):
             cols = cols_of(p)
 
-            @pl.when(stage < last)
-            def _():
-                b_copy(k, p).wait_recv()
+            if span == 1:
+
+                @pl.when(stage < last)
+                def _():
+                    b_copy(k, p).wait_recv()
 
             s_buf[0, rows, cols] = (
-                g_buf[rows, cols].astype(jnp.float32) * slopes[rows, cols]
+                g_buf[rows, cols].astype(jnp.float32) * slopes[rows, cols].astype(jnp.float32)
             ).astype(jnp.bfloat16)
-            s_copy(k, p).start()
-
-    def backward_own(k):
+            for q in range(span):
+                s_copy(k + q, p).start()
+
+    def backward_own(k, span):
         @pl.when(stage > 0)
         def _():
-            rows = rows_of(k)
-            acc[...] = mm(s_buf[0, rows, :], w_bwd[0])
-
-    def backward_rest(k):
-        rows = rows_of(k)
+            acc[pl.ds(0, span * CHUNK), :] = mm(s_buf[0, wide_rows(k, span), :], w_bwd[0])
+
+    def backward_rest(k, span):
+        rows, some = wide_rows(k, span), pl.ds(0, span * CHUNK)
         for p in range(PIECES):
-            s_copy(k, p).wait_recv()
+            for q in range(span):
+                s_copy(k + q, p).wait_recv()
             cols = cols_of(p)
             if p < PIECES - 1:
 
                 @pl.when(stage > 0)
                 def _():
-                    acc[...] += mm(s_buf[1, rows, cols], w_bwd[1, cols, :])
+                    acc[some, :] += mm(s_buf[1, rows, cols], w_bwd[1, cols, :])
 
         @pl.when(stage > 0)
         def _():
-            @pl.when(stage < last)
-            def _():
-                for p in range(PIECES):
-                    f_copy(k, p).wait_send()
+            if span == 1:
+
+                @pl.when(stage < last)
+                def _():
+                    for p in range(PIECES):
+                        f_copy(k, p).wait_send()
 
             for p in range(PIECES):
                 cols = cols_of(p)
-                back = acc[:, cols] + mm(s_buf[1, rows, end], w_bwd[1, end, cols])
+                back = acc[some, cols] + mm(s_buf[1, rows, end], w_bwd[1, end, cols])
                 h_send[rows, cols] = (
                     g_buf[rows, cols].astype(jnp.float32) + back
                 ).astype(jnp.bfloat16)
                 b_copy(k, p).start()
-
-    def backward_end(k):
-        @pl.when(lax.rem(k, 2) == core)
-        def _():
-            for d in range(2, CHIPS, 2):
-                sa_send(k, d).start()
-
-            @pl.when(jnp.logical_not(hold_s) | (k < HELD))
-            def _():
-                for d in range(1, CHIPS, 2):
-                    sa_send(k, d).start()
-
-            which = jnp.where(lax.rem(ring, 2) == core, 0, 1)
-            cols = pl.ds(pl.multiple_of(side * QUAD, QUAD), QUAD)
-            s_all[slot_of(k // 2, chip), :] = s_buf[which, rows_of(k), cols]
+            for q in range(1, span):
+                for p in range(PIECES):
+                    b_copy(k + q, p).start()
+
+    def backward_end(k, span):
+        for q in range(span):
+
+            @pl.when(lax.rem(k + q, 2) == core)
+            def _():
+                for d in range(2, CHIPS, 2):
+                    sa_send(k + q, d).start()
+
+                @pl.when(jnp.logical_not(hold_s) | (k + q < HELD))
+                def _():
+                    for d in range(1, CHIPS, 2):
+                        sa_send(k + q, d).start()
+
+                which = jnp.where(lax.rem(ring, 2) == core, 0, 1)
+                cols = pl.ds(pl.multiple_of(side * QUAD, QUAD), QUAD)
+                s_all[slot_of((k + q) // 2, chip), :] = s_buf[which, rows_of(k + q), cols]
+
+    def forward(k, span):
+        forward_own(k, span)
+        forward_rest(k, span)
+        forward_end(k, span)
+
+    def backward(k, span):
+        backward_start(k, span)
+        backward_own(k, span)
+        backward_rest(k, span)
+        backward_end(k, span)
 
     tile = 256
 
     def turn():
+        loads[2].wait()
+
         @pl.when(stage > 0)
         def _():
             def step(i, carry):
@@ -541,11 +571,13 @@
     ahead = jnp.where(stage == last, 1, jnp.where(stage == last - 1, AHEAD, CHUNKS))
 
     def slot(t, carry):
-        @pl.when(t < CHUNKS)
-        def _():
-            forward_own(t)
-            forward_rest(t)
-            forward_end(t)
+        kf = jnp.where(stage == last, jnp.where(t == 0, 0, CHUNKS - 1), t)
+        kb = jnp.where(stage == last, kf, t - (ahead - 1))
+        alone = (stage < last) | (t == 0) | (t == CHUNKS // 2)
+
+        @pl.when(alone & (kf < CHUNKS))
+        def _():
+            forward(kf, 1)
 
         @pl.when((t == CHUNKS - 1) & hold_x)
         def _():
@@ -568,13 +600,14 @@
         def _():
             collect_x()
 
-        @pl.when(t >= ahead - 1)
-        def _():
-            kb = t - (ahead - 1)
-            backward_start(kb)
-            backward_own(kb)
-            backward_rest(kb)
-            backward_end(kb)
+        @pl.when(alone & (kb >= 0))
+        def _():
+            backward(kb, 1)
+
+        @pl.when(jnp.logical_not(alone))
+        def _():
+            forward(2 * t - 1, 2)
+            backward(2 * t - 1, 2)
 
         return carry
 
@@ -582,7 +615,7 @@
     def _():
         turn()
 
-    lax.fori_loop(0, CHUNKS + ahead - 1, slot, 0)
+    lax.fori_loop(0, jnp.where(stage == last, CHUNKS // 2 + 1, CHUNKS + ahead - 1), slot, 0)
 
     @pl.when(hold_s)
     def _():
@@ -617,7 +650,7 @@
     def o_copy(n, j):
         owner = {"dp": (2 * upper + j // 2) * 4 + lax.rem(j, 2) * 2 + core}
         return remote(
-            o_send.at[n], o_recv.at[quarter], o_send_sem.at[n], o_recv_sem.at[quarter], owner
+            e_send.at[n], o_recv.at[quarter], o_send_sem.at[n], o_recv_sem.at[quarter], owner
         )
 
     def share(n, carry):
@@ -635,7 +668,8 @@
 
         @pl.when(n < 3)
         def _():
-            o_send[n] = whole
+            e_copy(n).wait_send()
+            e_send[n] = whole
             o_copy(n, j).start()
 
         @pl.when(n == 3)
@@ -739,8 +773,7 @@
 
     lax.fori_loop(1, 4, condition, 0)
 
-    for n in range(4):
-        e_copy(n).wait_send()
+    e_copy(3).wait_send()
     for n in range(3):
         o_copy(n, lax.rem(quarter + 1 + n, 4)).wait_send()
     for e in range(2):
@@ -770,18 +803,17 @@
             pltpu.VMEM((2, PAIR, HALF), bf16),
             pltpu.VMEM((2, PAIR, HALF), bf16),
             pltpu.VMEM((PAIR, HALF), bf16),
-            pltpu.VMEM((PAIR, HALF), f32),
+            pltpu.VMEM((PAIR, HALF), bf16),
             pltpu.VMEM((PAIR, HALF), bf16),
             pltpu.VMEM((2, HALF, HALF), bf16),
             pltpu.VMEM((2, HALF, HALF), bf16),
             pltpu.VMEM((HALF, HALF), bf16),
-            pltpu.VMEM((CHUNK, HALF), f32),
+            pltpu.VMEM((2 * CHUNK, HALF), f32),
             pltpu.VMEM((SEEN, HALF), bf16),
             pltpu.VMEM((HALF, SEEN), bf16),
             pltpu.VMEM((SEEN, QUAD), bf16),
             pltpu.VMEM((4, BLOCK, QUAD), bf16),
             pltpu.VMEM((4, BLOCK, QUAD), bf16),
-            pltpu.VMEM((3, BLOCK, QUAD), bf16),
             pltpu.VMEM((4, BLOCK, QUAD), bf16),
             pltpu.VMEM((2, BLOCK, BLOCK), f32),
             pltpu.VMEM((BLOCK, BLOCK), bf16),
@@ -808,10 +840,27 @@
     )(counts, tokens, cotangent, matrix, inverse_in, inverse_out)
 
 
+def hand_over(*refs):
+    for i in range(3):
+        refs[3 + i][...] = refs[i][...]
+
+
+def outputs(*arrays):
+    in_vmem = pl.BlockSpec(memory_space=pltpu.VMEM)
+    return pl.pallas_call(
+        hand_over,
+        out_shape=[jax.ShapeDtypeStruct(a.shape, a.dtype) for a in arrays],
+        in_specs=[in_vmem] * 3,
+        out_specs=[in_vmem] * 3,
+        name="outputs",
+    )(*arrays)
+
+
 def shards(tokens, cotangent, live_counts, weight, inverse_in, inverse_out):
-    update, owned_in, owned_out = run_pipeline(
+    results = run_pipeline(
         live_counts[0], tokens, cotangent, weight[0], inverse_in[0, 0], inverse_out[0]
     )
+    update, owned_in, owned_out = outputs(*results)
     return (update[None], owned_in[None, None], owned_out[None, None])
 
 

time: 200 us -> 194 us (0.970)
  local copies, waits for them, and re-layouts: 3.77 us -> 0 us
  Pallas kernels: 195 us -> 193 us
    pallas_call x1, Pallas kernels: 195 us -> 190 us  [run_pipeline(): pl.pallas_call(functools.partial(pipeline, lax.axis_size('section')), out...]
    unnamed x7 -> x0, local copies, waits for them, and re-layouts: 3.77 us -> none
    pallas_call x0 -> x1, Pallas kernels: none -> 2.54 us  [outputs(): pl.pallas_call(hand_over, out_shape=[jax.ShapeDtypeStruct(a.shape, a.dtyp...]
where the time goes in v6:
time: 194 us; the launch traced here: 193 us
  Pallas kernels  193 us (99%)
    pallas_call x1, Pallas kernels, run_pipeline(): pl.pallas_call(functools.partial(pipeline, lax.axis_size('section')), out...  190 us

profile of v6, /device:TPU:5, one launch (start us, length us, event | category | flops | bytes accessed | tf_op | source)
XLA Modules:
  0.0 193.2 jit_solution(10257880422725422076)
XLA Ops:
  0.6 190.0 %pipeline.1 = (bf16[192,3072]{1,0:T(8,128)(2,1)}, f32[192,192]{1,0:T(8,128)}, f32[192,192]{1,0:T(8,128)}) custom-call(s32[4]{0:T(128)} %bitcast.10, bf16[320,3072]{1,0:T(8,128)(2,1)} %tokens.1, bf16[320,3072]{1,0:T(8,128)(2,1)} %cotangent.1, bf16[3072,3072]{1,0:T(8,128)(2,1)} %bitcast.7, f32[192,192]{1,0:T(8,128)} %bitcast.9, f32[16,192,192]{2,1,0:T(8,128)} %bitcast.8), custom_call_target="tpu_custom_call" | custom-call | tf_op jit(solution)/shard_map/pipeline/pallas_call | solution.py:793
  190.7 2.5 %outputs.1 = (bf16[192,3072]{1,0:T(8,128)(2,1)}, f32[192,192]{1,0:T(8,128)}, f32[192,192]{1,0:T(8,128)}) custom-call(bf16[192,3072]{1,0:T(8,128)(2,1)} %get-tuple-element.9.refs_0_, f32[192,192]{1,0:T(8,128)} %get-tuple-element.10.refs_1_, f32[192,192]{1,0:T(8,128)} %get-tuple-element.11.refs_2_), custom_call_target="tpu_custom_call" | custom-call | tf_op jit(solution)/shard_map/outputs/pallas_call | solution.py:850

commit v7 on v6

--- a/solution.py
+++ b/solution.py
@@ -157,9 +157,6 @@
         pltpu.make_async_copy(weight.at[sib_cols, own_cols], w_fwd.at[1], load_sem.at[1]),
         pltpu.make_async_copy(weight.at[own_cols, sib_cols], w_raw, load_sem.at[2]),
     )
-    for load in loads[:2]:
-        load.start()
-
     @pl.when(stage == 0)
     def _():
         for move in fetch(tokens):
@@ -169,6 +166,9 @@
     def _():
         for move in fetch(cotangent):
             move.start()
+
+    for load in loads[:2]:
+        load.start()
 
     barrier = pltpu.get_barrier_semaphore()
 
@@ -475,13 +475,13 @@
 
             @pl.when(lax.rem(k + q, 2) == core)
             def _():
-                for d in range(2, CHIPS, 2):
-                    sa_send(k + q, d).start()
-
                 @pl.when(jnp.logical_not(hold_s) | (k + q < HELD))
                 def _():
-                    for d in range(1, CHIPS, 2):
+                    for d in (5, 3, 7, 1):
                         sa_send(k + q, d).start()
+
+                for d in (4, 2, 6):
+                    sa_send(k + q, d).start()
 
                 which = jnp.where(lax.rem(ring, 2) == core, 0, 1)
                 cols = pl.ds(pl.multiple_of(side * QUAD, QUAD), QUAD)
@@ -570,6 +570,11 @@
 
     ahead = jnp.where(stage == last, 1, jnp.where(stage == last - 1, AHEAD, CHUNKS))
 
+    def s_arrive(i, carry):
+        for d in range(1, CHIPS):
+            sa_recv(i, d).wait_recv()
+        return carry
+
     def slot(t, carry):
         kf = jnp.where(stage == last, jnp.where(t == 0, 0, CHUNKS - 1), t)
         kb = jnp.where(stage == last, kf, t - (ahead - 1))
@@ -600,6 +605,10 @@
         def _():
             collect_x()
 
+        @pl.when((stage == 0) & (kb == CHUNKS - 1))
+        def _():
+            lax.fori_loop(0, SHARE - 2, s_arrive, 0)
+
         @pl.when(alone & (kb >= 0))
         def _():
             backward(kb, 1)
@@ -633,12 +642,7 @@
     def _():
         collect_x()
 
-    def arrive(i, carry):
-        for d in range(1, CHIPS):
-            sa_recv(i, d).wait_recv()
-        return carry
-
-    lax.fori_loop(0, SHARE, arrive, 0)
+    lax.fori_loop(jnp.where(stage == 0, SHARE - 2, 0), SHARE, s_arrive, 0)
 
     def block(j, parity):
         rows = pl.ds(pl.multiple_of((2 * j + parity) * BLOCK, 16), BLOCK)

time: 194 us -> 192 us (0.990)
  Pallas kernels: 193 us -> 191 us
    pallas_call x1, Pallas kernels: 190 us -> 188 us  [run_pipeline(): pl.pallas_call(functools.partial(pipeline, lax.axis_size('section')), out...]
where the time goes in v7:
time: 192 us; the launch traced here: 191 us
  Pallas kernels  191 us (99%)
    pallas_call x1, Pallas kernels, run_pipeline(): pl.pallas_call(functools.partial(pipeline, lax.axis_size('section')), out...  188 us

profile of v7, /device:TPU:5, one launch (start us, length us, event | category | flops | bytes accessed | tf_op | source)
XLA Modules:
  0.0 191.2 jit_solution(3661219665019736211)
XLA Ops:
  0.6 188.0 %pipeline.1 = (bf16[192,3072]{1,0:T(8,128)(2,1)}, f32[192,192]{1,0:T(8,128)}, f32[192,192]{1,0:T(8,128)}) custom-call(s32[4]{0:T(128)} %bitcast.10, bf16[320,3072]{1,0:T(8,128)(2,1)} %tokens.1, bf16[320,3072]{1,0:T(8,128)(2,1)} %cotangent.1, bf16[3072,3072]{1,0:T(8,128)(2,1)} %bitcast.7, f32[192,192]{1,0:T(8,128)} %bitcast.9, f32[16,192,192]{2,1,0:T(8,128)} %bitcast.8), custom_call_target="tpu_custom_call" | custom-call | tf_op jit(solution)/shard_map/pipeline/pallas_call | solution.py:797
  188.6 2.5 %outputs.1 = (bf16[192,3072]{1,0:T(8,128)(2,1)}, f32[192,192]{1,0:T(8,128)}, f32[192,192]{1,0:T(8,128)}) custom-call(bf16[192,3072]{1,0:T(8,128)(2,1)} %get-tuple-element.9.refs_0_, f32[192,192]{1,0:T(8,128)} %get-tuple-element.10.refs_1_, f32[192,192]{1,0:T(8,128)} %get-tuple-element.11.refs_2_), custom_call_target="tpu_custom_call" | custom-call | tf_op jit(solution)/shard_map/outputs/pallas_call | solution.py:854
